TPU v7x, 32 devices: a whole 2x2x4 slice. The times are simulated.
32 devices in a mesh: groups: 2 (over y), tile: 8 (over z, x), cuts: 2 (over core).
Axes of the slice: x: 2, y: 2, z: 4, core: 2. Of those that a mesh axis runs over, the one named last changes fastest.
Arguments:
- slice_rows: float32 [8192, 512], P(('groups', 'tile', 'cuts')), parts along dimension 0, may hold values from -0.025625 to 0.025625
- row_owner: int32 [8192, 1], P(('groups', 'tile', 'cuts')), parts along dimension 0, may hold values from 0 to 7; in each aligned block of 256 rows (0 to 255, 256 to 511, ...) at most 48 rows name the same one
- leaf_row: int32 [8192], P(('groups', 'tile', 'cuts')), parts along dimension 0, may hold values from 0 to 511
- exponent: int32 [8192], P(('groups', 'tile', 'cuts')), parts along dimension 0, may hold values from -1 to 1
- environment: float32 [16384, 512], P(('groups', 'tile', 'cuts')), parts along dimension 0, may hold values from -0.25 to 0.25
- ordering: int32 [32, 512], P(('groups', 'tile', 'cuts')), parts along dimension 0, may hold values from 0 to 511, each once within a row
- sign_mask: int32 [32, 512], P(('groups', 'tile', 'cuts')), parts along dimension 0, may hold values 0 or 1
Outputs:
- partition: float32 [1024, 512], P(('groups', 'tile'), 'cuts'), parts along dimension 0
- log_scale: float32 [2], P('groups'), parts along dimension 0
There are 2 independent parts, one for each index of `groups`. A program takes and returns all parts, laid end to end along the dimension named above; each array names one. Nothing has to cross between parts.
Inputs may be any that keep to these rules, and one draw needn't show every extreme that they name: `row_owner`: of the rows of one device at most 48 name the same owner, and in some device exactly 48 do.
All inputs are finite; a program needn't handle non-finite values. No bound on the sum of `sign_mask` on one device may be relied on, other than what follows from the above.
Results may differ from a plain program's by a relative error of at most 0.0003.
Values sent between devices are 32-bit elements; how exact they have to be, the bound alone decides.
A program may use at most 64 MiB of HBM per device.

v0:
```python
import jax
import jax.numpy as jnp
from jax import lax
from jax.sharding import PartitionSpec as P


def from_partner(x, axis, bit):
    return lax.ppermute(x, axis, [(i, i ^ 1 << bit) for i in range(lax.axis_size(axis))])


def multiply(left_factor, right_factor):
    return jnp.dot(
        left_factor,
        right_factor,
        precision=lax.Precision.HIGHEST,
        preferred_element_type=jnp.float32,
    )


def body(slice_rows, row_owner, leaf_row, exponent, environment, ordering, sign_mask):
    tiles = lax.axis_size("tile")
    cut_count = lax.axis_size("cuts")
    width = slice_rows.shape[1]
    row_count = slice_rows.shape[0]
    capacity = max(2, (3 * row_count + 2 * tiles - 1) // (2 * tiles))
    factor = jnp.where(exponent == -1, 0.5, jnp.where(exponent == 1, 2.0, 1.0)).astype(jnp.float32)
    scaled = slice_rows * factor[:, None]
    owners = row_owner[:, 0]
    hits = (owners[:, None] == jnp.arange(tiles, dtype=jnp.int32)[None, :]).astype(jnp.int32)
    before = jnp.cumsum(hits, axis=0) - hits
    position = jnp.sum(before * hits, axis=1)
    placed = owners * capacity + position
    outgoing = jnp.zeros((tiles * capacity, width), jnp.float32).at[placed].set(scaled)
    outgoing_rows = jnp.zeros((tiles * capacity,), jnp.int32).at[placed].set(leaf_row)
    arrived, arrived_rows = (
        lax.all_to_all(outgoing, "tile", split_axis=0, concat_axis=0, tiled=True),
        lax.all_to_all(outgoing_rows, "tile", split_axis=0, concat_axis=0, tiled=True),
    )
    collected = jnp.zeros((width, width), jnp.float32).at[arrived_rows].add(arrived)
    contracted = multiply(collected, environment)
    columns = jnp.arange(width, dtype=jnp.int32)
    signs = 1.0 - 2.0 * sign_mask[0].astype(jnp.float32)
    signed = (ordering[0][:, None] == columns[None, :]).astype(jnp.float32) * signs[:, None]
    product = contracted + signed
    for level in range(tiles.bit_length() - 1):
        partner = from_partner(product, "tile", level)
        upper = lax.axis_index("tile") >> level & 1 == 1
        first_part = jnp.where(upper, partner, product)
        second_part = jnp.where(upper, product, partner)
        product = multiply(first_part, second_part)
    level = 0
    partner = from_partner(product, "cuts", level)
    upper = lax.axis_index("cuts") >> level & 1 == 1
    first_part = jnp.where(upper, partner, product)
    second_part = jnp.where(upper, product, partner)
    product = multiply(first_part, second_part)
    spread = jnp.sqrt(jnp.mean(product * product) + 1e-06)
    rows_each = width // tiles
    cols_each = width // cut_count
    row_start = lax.axis_index("tile") * rows_each
    col_start = lax.axis_index("cuts") * cols_each
    own_block = lax.dynamic_slice(product, (row_start, col_start), (rows_each, cols_each))
    return (own_block / spread, jnp.log(spread).reshape(1))


def solution(mesh):
    return jax.shard_map(
        body,
        mesh=mesh,
        in_specs=(
            P(("groups", "tile", "cuts"), None),
            P(("groups", "tile", "cuts"), None),
            P(("groups", "tile", "cuts")),
            P(("groups", "tile", "cuts")),
            P(("groups", "tile", "cuts"), None),
            P(("groups", "tile", "cuts"), None),
            P(("groups", "tile", "cuts"), None),
        ),
        out_specs=(P(("groups", "tile"), "cuts"), P("groups")),
        check_vma=False,
    )
```

profile of v0, /device:TPU:0, one launch (start us, length us, event | category | flops | bytes accessed | tf_op | source)
XLA Modules:
  0.0 158.7 jit_solution(14111099245107817277)
XLA Ops:
  0.6 0.0 copy-start
  0.6 0.0 copy-start.2
  0.7 0.8 copy-done.2
  1.4 0.6 reduce-window.6
  2.0 0.2 slice_reduce_fusion
  2.2 0.1 fusion.23
  2.3 1.6 scatter_custom_fusion
  3.9 0.7 all_to_all.16
  4.6 0.0 copy-start.5
  4.6 7.4 %all-to-all-start = ((s32[8,48,1]{1,2,0:T(1,128)}), s32[8,48,1]{1,2,0:T(1,128)S(1)}, u32[]{:S(2)}, u32[]{:S(2)}) async-start(s32[8,48,1]{1,2,0:T(1,128)} %bitcast.6), calls=%async_computation | async-start | bytes 8192 | tf_op jit(solution)/shard_map/all_to_all | solution.py:37
  12.0 0.0 copy-done.5
  12.0 2.9 %scatter_custom_fusion.1 = f32[384,512]{1,0:T(8,128)} fusion(s32[256]{0:T(256)S(1)} %bitcast.28, f32[256,512]{1,0:T(8,128)} %param.7, f32[]{:T(128)} %constant.22.clone.1, f32[256]{0:T(256)S(1)} %compare_select_fusion.3), kind=kCustom, calls=%fused_computation.18 | custom fusion | flops 131072 | bytes 1311748 | tf_op jit(solution)/shard_map/scatter | solution.py:33
  14.9 3.5 %all-to-all-done = s32[8,48,1]{1,2,0:T(1,128)S(1)} async-done(((s32[8,48,1]{1,2,0:T(1,128)}), s32[8,48,1]{1,2,0:T(1,128)S(1)}, u32[]{:S(2)}, u32[]{:S(2)}) %all-to-all-start) | async-done | bytes 1568 | tf_op jit(solution)/shard_map/all_to_all | solution.py:37
  18.4 0.0 copy-start.4
  18.4 3.7 %all-to-all-start.1 = ((f32[8,48,512]{2,1,0:T(8,128)}), f32[8,48,512]{2,1,0:T(8,128)S(1)}, u32[]{:S(2)}, u32[]{:S(2)}) async-start(f32[8,48,512]{2,1,0:T(8,128)} %bitcast.7), calls=%async_computation.1 | async-start | bytes 1572864 | tf_op jit(solution)/shard_map/all_to_all | solution.py:36
  22.0 0.0 copy-done.4
  22.1 0.5 broadcast.74
  22.6 0.7 reduce.7
  23.3 0.1 all_to_all.18
  23.4 17.7 %all-to-all-done.1 = f32[8,48,512]{2,1,0:T(8,128)S(1)} async-done(((f32[8,48,512]{2,1,0:T(8,128)}), f32[8,48,512]{2,1,0:T(8,128)S(1)}, u32[]{:S(2)}, u32[]{:S(2)}) %all-to-all-start.1) | async-done | bytes 786464 | tf_op jit(solution)/shard_map/all_to_all | solution.py:36
  41.1 3.3 %scatter_custom_fusion.2 = f32[512,512]{1,0:T(8,128)S(1)} fusion(s32[384]{0:T(512)S(1)} %fusion.25, f32[384,512]{1,0:T(8,128)S(1)} %bitcast.21, f32[]{:T(128)} %constant.22.clone.1), kind=kCustom, calls=%fused_computation.20 | custom fusion | flops 196608 | bytes 1048580 | tf_op jit(solution)/shard_map/scatter-add | solution.py:39
  44.3 0.0 copy-start.3
  44.3 0.0 copy-done
  44.4 0.7 copy-done.3
  45.0 1.9 %convolution_add_fusion = f32[512,512]{1,0:T(8,128)S(1)} fusion(f32[512,512]{1,0:T(8,128)S(1)} %scatter_custom_fusion.2, f32[512,512]{1,0:T(8,128)S(1)} %copy-done, f32[512]{0:T(512)S(1)} %bitcast.24, s32[512]{0:T(512)S(1)} %bitcast.26), kind=kOutput, calls=%fused_computation.3 | convolution fusion | flops 1611399168 | bytes 3149824 | tf_op jit(solution)/shard_map/dot_general | solution.py:12
  46.9 1.5 collective-permute-start
  48.4 22.0 %collective-permute-done = f32[512,512]{1,0:T(8,128)} collective-permute-done((f32[512,512]{1,0:T(8,128)S(1)}, f32[512,512]{1,0:T(8,128)}, u32[]{:S(2)}, u32[]{:S(2)}) %collective-permute-start) | collective-permute-done | bytes 1048608 | tf_op jit(solution)/shard_map/ppermute | solution.py:8
  70.4 3.1 %fusion.9 = f32[512,512]{1,0:T(8,128)S(1)} fusion(f32[512,512]{1,0:T(8,128)S(1)} %convolution_add_fusion, f32[512,512]{1,0:T(8,128)} %collective-permute-done, pred[]{:T(512)S(6)} %eq.67), kind=kOutput, calls=%fused_computation.14 | convolution fusion | flops 1611137024 | bytes 3145729 | tf_op jit(solution)/shard_map/dot_general | solution.py:12
  73.6 0.0 copy-start.1
  73.6 0.1 collective-permute-start.1
  73.7 0.9 copy-done.1
  74.6 21.5 %collective-permute-done.1 = f32[512,512]{1,0:T(8,128)S(1)} collective-permute-done((f32[512,512]{1,0:T(8,128)S(1)}, f32[512,512]{1,0:T(8,128)S(1)}, u32[]{:S(2)}, u32[]{:S(2)}) %collective-permute-start.1) | collective-permute-done | bytes 1048608 | tf_op jit(solution)/shard_map/ppermute | solution.py:8
  96.1 3.1 %fusion.6 = f32[512,512]{1,0:T(8,128)S(1)} fusion(f32[512,512]{1,0:T(8,128)} %copy-done.1, f32[512,512]{1,0:T(8,128)S(1)} %collective-permute-done.1, pred[]{:T(512)S(6)} %eq.66), kind=kOutput, calls=%fused_computation.11 | convolution fusion | flops 1611137024 | bytes 3145729 | tf_op jit(solution)/shard_map/dot_general | solution.py:12
  99.2 2.8 %collective-permute-start.2 = (f32[512,512]{1,0:T(8,128)S(1)}, f32[512,512]{1,0:T(8,128)}, u32[]{:S(2)}, u32[]{:S(2)}) collective-permute-start(f32[512,512]{1,0:T(8,128)S(1)} %fusion.6), channel_id=1, source_target_pairs={{0,8},{2,10},{4,12},{6,14},{8,0},{10,2},{12,4},{14,6},{1,9},{3,11}... | collective-permute-start | bytes 3145736 | tf_op jit(solution)/shard_map/ppermute | solution.py:8
  102.0 44.0 %collective-permute-done.2 = f32[512,512]{1,0:T(8,128)} collective-permute-done((f32[512,512]{1,0:T(8,128)S(1)}, f32[512,512]{1,0:T(8,128)}, u32[]{:S(2)}, u32[]{:S(2)}) %collective-permute-start.2) | collective-permute-done | bytes 1048608 | tf_op jit(solution)/shard_map/ppermute | solution.py:8
  146.0 3.1 %fusion.3 = f32[512,512]{1,0:T(8,128)S(1)} fusion(f32[512,512]{1,0:T(8,128)S(1)} %fusion.6, f32[512,512]{1,0:T(8,128)} %collective-permute-done.2, pred[]{:T(512)S(6)} %eq.65), kind=kOutput, calls=%fused_computation.8 | convolution fusion | flops 1611137024 | bytes 3145729 | tf_op jit(solution)/shard_map/dot_general | solution.py:12
  149.2 0.1 collective-permute-start.3
  149.2 2.6 %collective-permute-done.3 = f32[512,512]{1,0:T(8,128)S(1)} collective-permute-done((f32[512,512]{1,0:T(8,128)S(1)}, f32[512,512]{1,0:T(8,128)S(1)}, u32[]{:S(2)}, u32[]{:S(2)}) %collective-permute-start.3) | collective-permute-done | bytes 1048608 | tf_op jit(solution)/shard_map/ppermute | solution.py:8
  151.9 3.5 %multiply_reduce_fusion = (f32[]{:T(128)}, f32[512,512]{1,0:T(8,128)}) fusion(f32[512,512]{1,0:T(8,128)S(1)} %fusion.3, f32[512,512]{1,0:T(8,128)S(1)} %collective-permute-done.3, pred[]{:T(512)S(6)} %eq.64), kind=kOutput, calls=%fused_computation.4 | convolution fusion | flops 1611661312 | bytes 3145733 | tf_op jit(solution)/shard_map/dot_general | solution.py:12
  156.1 1.5 dynamic-slice_divide_fusion
  (7 shorter events, 0.1 us)
Async XLA Ops:
  0.6 43.7 %copy-start = (f32[512,512]{1,0:T(8,128)S(1)}, f32[512,512]{1,0:T(8,128)}, u32[]{:S(2)}) copy-start(f32[512,512]{1,0:T(8,128)} %param.11) | copy-start | bytes 3145732
  0.6 0.8 copy-start.2
  4.6 7.4 %copy-start.5 = (s32[256]{0:T(256)S(1)}, s32[256]{0:T(256)}, u32[]{:S(2)}) copy-start(s32[256]{0:T(256)} %param.10) | copy-start | bytes 3076
  4.6 13.8 %all-to-all-start = ((s32[8,48,1]{1,2,0:T(1,128)}), s32[8,48,1]{1,2,0:T(1,128)S(1)}, u32[]{:S(2)}, u32[]{:S(2)}) async-start(s32[8,48,1]{1,2,0:T(1,128)} %bitcast.6), calls=%async_computation | async-start | bytes 8192 | tf_op jit(solution)/shard_map/all_to_all | solution.py:37
  18.4 3.7 %copy-start.4 = (s32[1,512]{1,0:T(1,128)S(1)}, s32[1,512]{1,0:T(1,128)}, u32[]{:S(2)}) copy-start(s32[1,512]{1,0:T(1,128)} %param.13) | copy-start | bytes 6148
  18.4 22.7 %all-to-all-start.1 = ((f32[8,48,512]{2,1,0:T(8,128)}), f32[8,48,512]{2,1,0:T(8,128)S(1)}, u32[]{:S(2)}, u32[]{:S(2)}) async-start(f32[8,48,512]{2,1,0:T(8,128)} %bitcast.7), calls=%async_computation.1 | async-start | bytes 1572864 | tf_op jit(solution)/shard_map/all_to_all | solution.py:36
  44.3 0.7 copy-start.3
  46.9 23.5 %collective-permute-start = (f32[512,512]{1,0:T(8,128)S(1)}, f32[512,512]{1,0:T(8,128)}, u32[]{:S(2)}, u32[]{:S(2)}) collective-permute-start(f32[512,512]{1,0:T(8,128)S(1)} %convolution_add_fusion), channel_id=1, source_target_pairs={{0,2},{2,0},{4,6},{6,4},{8,10},{10,8},{12,14},{14,12},{1,3},{3,1},... | collective-permute-start | bytes 3145736 | tf_op jit(solution)/shard_map/ppermute | solution.py:8
  73.6 1.0 copy-start.1
  73.6 22.5 %collective-permute-start.1 = (f32[512,512]{1,0:T(8,128)S(1)}, f32[512,512]{1,0:T(8,128)S(1)}, u32[]{:S(2)}, u32[]{:S(2)}) collective-permute-start(f32[512,512]{1,0:T(8,128)S(1)} %fusion.9), channel_id=1, source_target_pairs={{0,4},{2,6},{4,0},{6,2},{8,12},{10,14},{12,8},{14,10},{1,5},{3,7},... | collective-permute-start | bytes 3145736 | tf_op jit(solution)/shard_map/ppermute | solution.py:8
  99.2 46.8 %collective-permute-start.2 = (f32[512,512]{1,0:T(8,128)S(1)}, f32[512,512]{1,0:T(8,128)}, u32[]{:S(2)}, u32[]{:S(2)}) collective-permute-start(f32[512,512]{1,0:T(8,128)S(1)} %fusion.6), channel_id=1, source_target_pairs={{0,8},{2,10},{4,12},{6,14},{8,0},{10,2},{12,4},{14,6},{1,9},{3,11}... | collective-permute-start | bytes 3145736 | tf_op jit(solution)/shard_map/ppermute | solution.py:8
  149.2 2.7 %collective-permute-start.3 = (f32[512,512]{1,0:T(8,128)S(1)}, f32[512,512]{1,0:T(8,128)S(1)}, u32[]{:S(2)}, u32[]{:S(2)}) collective-permute-start(f32[512,512]{1,0:T(8,128)S(1)} %fusion.3), channel_id=1, source_target_pairs={{0,1},{1,0},{2,3},{3,2},{4,5},{5,4},{6,7},{7,6},{8,9},{9,8},{10,11... | collective-permute-start | bytes 3145736 | tf_op jit(solution)/shard_map/ppermute | solution.py:8
where the time goes:
time: 159 us
  waiting for transfers between devices  111 us (70%)
  starting transfers between devices  15.5 us (10%)
  matrix products  14.7 us (9%)
  other arithmetic  9.06 us (6%)
  local copies, waits for them, and re-layouts  5.38 us (3%)
  between operations  2.67 us (2%)
    ppermute x4, waiting for transfers between devices, from_partner(): lax.ppermute(x, axis, [(i, i ^ 1 << bit) for i in range(lax.axis_size(axi...  90.2 us
    all_to_all x1, waiting for transfers between devices, body(): lax.all_to_all(outgoing, 'tile', split_axis=0, concat_axis=0, tiled=True)  17.7 us
    dot_general x5, matrix products, multiply(): jnp.dot(left_factor, right_factor, precision=lax.Precision.HIGHEST, prefe...  14.7 us
    all_to_all x1, starting transfers between devices, body(): lax.all_to_all(outgoing_rows, 'tile', split_axis=0, concat_axis=0, tiled=...  7.38 us
    ppermute x4, starting transfers between devices, from_partner(): lax.ppermute(x, axis, [(i, i ^ 1 << bit) for i in range(lax.axis_size(axi...  4.44 us
    all_to_all x1, starting transfers between devices, body(): lax.all_to_all(outgoing, 'tile', split_axis=0, concat_axis=0, tiled=True)  3.68 us
    all_to_all x1, waiting for transfers between devices, body(): lax.all_to_all(outgoing_rows, 'tile', split_axis=0, concat_axis=0, tiled=...  3.47 us
    scatter-add x1, other arithmetic, body(): jnp.zeros((width, width), jnp.float32).at[arrived_rows].add(arrived)  3.26 us
  transfers between devices with their start and end apart: 6, of which 6 were waited for; matrix products, arithmetic and copies ran while one was open for 3% of the time, Pallas kernels for 0%

commit v1 on v0

--- a/solution.py
+++ b/solution.py
@@ -1,7 +1,361 @@
+import functools
+
 import jax
 import jax.numpy as jnp
 from jax import lax
+from jax.experimental import pallas as pl
+from jax.experimental.pallas import tpu as pltpu
 from jax.sharding import PartitionSpec as P
+
+MESH = pl.DeviceIdType.MESH
+F32, BF16 = jnp.float32, jnp.bfloat16
+NN = (((1,), (0,)), ((), ()))
+NT = (((1,), (1,)), ((), ()))
+
+
+def halves(x):
+    high = x.astype(BF16)
+    return high, (x - high.astype(F32)).astype(BF16)
+
+
+def dot(a, b, dims=NN):
+    return lax.dot_general(a, b, dims, preferred_element_type=F32)
+
+
+def dot3(left, right, dims=NN):
+    return (dot(left[0], right[1], dims) + dot(left[1], right[0], dims)) + dot(left[0], right[0], dims)
+
+
+def kernel(tiles, cap,
+           rows_ref, owner_ref, leaf_row_ref, exponent_ref, env_ref, ordering_ref, sign_ref,
+           block_ref, square_ref,
+           out_rows, out_ids, in_rows, in_ids, own, own_high, own_low, chain_high, chain_low,
+           pair_in, chain_in, chain_out, p_in, q_in, sums_out, sums_in,
+           route_send, route_recv, pair_send, pair_recv, chain_send, chain_recv,
+           p_send, p_recv, pass_send, pass_recv, q_send, q_recv, half_send, sum_send, sum_recv):
+    group, me, cut = lax.axis_index("groups"), lax.axis_index("tile"), lax.axis_index("cuts")
+    rows, width = rows_ref.shape
+    step = width // tiles
+    half = tiles // 2
+    slots = tiles * cap
+    count = 2 * tiles
+    ident = me * 2 + cut
+    place = jnp.where(cut == 0, me, tiles - 1 - me)
+    way = 1 - 2 * cut
+    last = place == tiles - 1
+
+    def chunk(ref, k):
+        return ref.at[pl.ds(pl.multiple_of(k * step, 8), step)]
+
+    def remote(src, dst, send, recv, tile, other):
+        return pltpu.make_async_remote_copy(
+            src_ref=src, dst_ref=dst, send_sem=send, recv_sem=recv,
+            device_id=(group, tile, other), device_id_type=MESH)
+
+    barrier = pltpu.get_barrier_semaphore()
+
+    @pl.loop(1, count)
+    def _(d):
+        peer = lax.rem(ident + d, count)
+        pl.semaphore_signal(barrier, inc=1, device_id=(group, peer // 2, lax.rem(peer, 2)), device_id_type=MESH)
+
+    square = 128 * ((rows + 127) // 128)
+    level = exponent_ref[...]
+    factor = jnp.where(level == -1, 0.5, jnp.where(level == 1, 2.0, 1.0)).astype(F32)
+    factor = jnp.broadcast_to(factor, (128, rows)).T[:, 0:1]
+    scaled = rows_ref[...] * factor
+    owner = owner_ref[...]
+    hits = (owner == lax.broadcasted_iota(jnp.int32, (rows, 128), 1)).astype(F32)
+    earlier = (lax.broadcasted_iota(jnp.int32, (rows, rows), 1)
+               < lax.broadcasted_iota(jnp.int32, (rows, rows), 0)).astype(F32)
+    before = dot(earlier.astype(BF16), hits.astype(BF16))
+    position = jnp.sum(before * hits, axis=1, keepdims=True)
+    position = jnp.broadcast_to(position, (rows, 128)).T[0:1, :].astype(jnp.int32)
+    owner = jnp.broadcast_to(owner.astype(F32), (rows, 128)).T[0:1, :].astype(jnp.int32)
+    slot = lax.broadcasted_iota(jnp.int32, (slots, rows), 0)
+    pick = (slot == owner * cap + position).astype(F32).astype(BF16)
+    high = scaled.astype(BF16)
+    rest = scaled - high.astype(F32)
+    middle = rest.astype(BF16)
+    low = (rest - middle.astype(F32)).astype(BF16)
+    out_rows[...] = (dot(pick, low) + dot(pick, middle)) + dot(pick, high)
+    seat = (slot == me * cap + position).astype(F32).astype(BF16)
+    named = jnp.where(lax.broadcasted_iota(jnp.int32, (tiles, rows), 0) == owner,
+                      leaf_row_ref[...] + 1, 0).astype(F32)
+    named_high, named_low = halves(named)
+    ids = dot(named_high, seat, NT) + dot(named_low, seat, NT)
+    for t in range(tiles):
+        out_ids[t] = ids[t:t + 1, :]
+
+    pl.semaphore_wait(barrier, count - 1)
+
+    def slots_of(ref, t):
+        return ref.at[pl.ds(pl.multiple_of(t * cap, 8), cap)]
+
+    def route(to, source):
+        return (remote(slots_of(out_rows, to), slots_of(in_rows, source), route_send.at[0, to],
+                       route_recv.at[0, source], to, cut),
+                remote(out_ids.at[to], in_ids.at[source], route_send.at[1, to],
+                       route_recv.at[1, source], to, cut))
+
+    @pl.loop(1, tiles)
+    def _(d):
+        for copy in route(lax.rem(me + d, tiles), me):
+            copy.start()
+
+    mine = pl.ds(pl.multiple_of(me * cap, 8), cap)
+    in_rows[mine] = out_rows[mine]
+    in_ids[me] = out_ids[me]
+    bond = jnp.where(lax.broadcasted_iota(jnp.int32, (width, width), 0) == ordering_ref[...],
+                     (1 - 2 * sign_ref[...]).astype(F32), 0.0)
+
+    @pl.when(cut == 0)
+    def _():
+        own[...] = bond.T
+        own_high[...], own_low[...] = halves(env_ref[...])
+
+    @pl.when(cut == 1)
+    def _():
+        own[...] = bond
+        own_high[...], own_low[...] = halves(env_ref[...].T)
+
+    @pl.loop(1, tiles)
+    def _(d):
+        source = lax.rem(me + d, tiles)
+        for copy in route(source, source):
+            copy.wait_recv()
+
+    wanted = jnp.sum(in_ids[...], axis=0).astype(jnp.int32) - 1
+    spread_out = (lax.broadcasted_iota(jnp.int32, (width, slots), 0) == wanted).astype(F32).astype(BF16)
+    in_high, in_low = halves(in_rows[...])
+    collected = halves(dot(spread_out, in_low) + dot(spread_out, in_high))
+
+    @pl.when(cut == 0)
+    def _():
+        own[...] += dot3(collected, (own_high[...], own_low[...]))
+
+    @pl.when(cut == 1)
+    def _():
+        own[...] += dot3((own_high[...], own_low[...]), collected, NT)
+
+    def pair(k):
+        return remote(chunk(own, k), chunk(pair_in, k), pair_send.at[k], pair_recv.at[k], me + way, cut)
+
+    def link(k):
+        return remote(chunk(chain_out, k), chunk(chain_in, k), chain_send.at[k], chain_recv.at[k],
+                      lax.rem(me + 2 * way + tiles, tiles), cut)
+
+    def p_copy(k):
+        return remote(chunk(chain_out, k), p_in, p_send.at[k], p_recv.at[0], k, 0)
+
+    def q_along(k):
+        return remote(chunk(q_in, k), chunk(q_in, k), q_send.at[0, k], q_recv.at[k], lax.rem(me + 2, tiles), cut)
+
+    def q_across(k):
+        return remote(chunk(q_in, k), chunk(q_in, k), q_send.at[1, k], q_recv.at[k], lax.rem(me + 1, tiles), cut)
+
+    def q_half(k):
+        return remote(chunk(chain_out, k), chunk(q_in, k), half_send.at[k], q_recv.at[k], 0, 0)
+
+    even_tile = lax.rem(me, 2) == 0
+    even_place = lax.rem(place, 2) == 0
+    p_root = jnp.logical_and(last, cut == 0)
+    q_root = jnp.logical_and(last, cut == 1)
+
+    def emit(k, value):
+        at = pl.ds(pl.multiple_of(k * step, 8), step)
+
+        @pl.when(jnp.logical_not(last))
+        def _():
+            chain_out[at] = value
+            link(k).start()
+
+        @pl.when(p_root)
+        def _():
+            @pl.when(k < tiles - 1)
+            def _():
+                chain_out[at] = value
+                p_copy(k).start()
+
+            @pl.when(k == tiles - 1)
+            def _():
+                p_in[...] = value
+
+        @pl.when(q_root)
+        def _():
+            @pl.when(k < half)
+            def _():
+                chain_out[at] = value
+                q_half(k).start()
+
+            @pl.when(k >= half)
+            def _():
+                q_in[pl.ds(pl.multiple_of((k - half) * step, 8), step)] = value
+                q_along(k - half).start()
+                q_across(k - half).start()
+
+    @pl.when(even_place)
+    def _():
+        @pl.loop(0, tiles)
+        def _(k):
+            pair(k).start()
+
+    @pl.when(jnp.logical_not(even_place))
+    def _():
+        own_high[...], own_low[...] = halves(own[...])
+
+        @pl.loop(0, tiles)
+        def _(k):
+            at = pl.ds(pl.multiple_of(k * step, 8), step)
+            pair(k).wait_recv()
+            value = dot3(halves(pair_in[at]), (own_high[...], own_low[...]))
+
+            @pl.when(place == 1)
+            def _():
+                emit(k, value)
+
+            @pl.when(place > 1)
+            def _():
+                chain_high[at], chain_low[at] = halves(value)
+
+        @pl.when(place > 1)
+        def _():
+            @pl.loop(0, tiles)
+            def _(k):
+                at = pl.ds(pl.multiple_of(k * step, 8), step)
+                link(k).wait_recv()
+                emit(k, dot3(halves(chain_in[at]), (chain_high[...], chain_low[...])))
+
+    @pl.when(jnp.logical_not(q_root))
+    def _():
+        @pl.loop(0, half)
+        def _(k):
+            q_half(k).wait_recv()
+
+            @pl.when(even_tile)
+            def _():
+                @pl.when(me < tiles - 2)
+                def _():
+                    q_along(k).start()
+
+                q_across(k).start()
+
+    def p_pass():
+        return remote(p_in, p_in, pass_send.at[0], pass_recv.at[0], me, 1)
+
+    @pl.when(cut == 0)
+    def _():
+        @pl.when(jnp.logical_not(p_root))
+        def _():
+            p_copy(0).wait_recv()
+
+        p_pass().start()
+
+    @pl.when(cut == 1)
+    def _():
+        p_pass().wait_recv()
+
+    result = dot3(halves(p_in[...]), halves(q_in[...]), NT)
+    block_ref[...] = result
+    total = jnp.sum(jnp.sum(result * result, axis=0, keepdims=True), axis=1, keepdims=True)
+    total = jnp.broadcast_to(total, (8, 128))
+    sums_out[...] = total
+
+    def share(peer, slot):
+        return remote(sums_out, sums_in.at[slot], sum_send.at[peer], sum_recv.at[slot],
+                      peer // 2, lax.rem(peer, 2))
+
+    @pl.loop(1, count)
+    def _(d):
+        share(lax.rem(ident + d, count), ident).start()
+
+    sums_in[ident] = total
+
+    @pl.loop(1, tiles)
+    def _(d):
+        for copy in route(lax.rem(me + d, tiles), me):
+            copy.wait_send()
+
+    @pl.when(even_place)
+    def _():
+        @pl.loop(0, tiles)
+        def _(k):
+            pair(k).wait_send()
+
+    @pl.when(jnp.logical_and(jnp.logical_not(even_place), jnp.logical_not(last)))
+    def _():
+        @pl.loop(0, tiles)
+        def _(k):
+            link(k).wait_send()
+
+    @pl.when(p_root)
+    def _():
+        @pl.loop(0, tiles - 1)
+        def _(k):
+            p_copy(k).wait_send()
+
+    @pl.when(q_root)
+    def _():
+        @pl.loop(0, half)
+        def _(k):
+            q_half(k).wait_send()
+
+    @pl.when(even_tile)
+    def _():
+        @pl.loop(0, half)
+        def _(k):
+            @pl.when(me < tiles - 2)
+            def _():
+                q_along(k).wait_send()
+
+            q_across(k).wait_send()
+
+    @pl.when(cut == 0)
+    def _():
+        p_pass().wait_send()
+
+    @pl.loop(1, count)
+    def _(d):
+        peer = lax.rem(ident + d, count)
+        share(peer, peer).wait_recv()
+        share(peer, peer).wait_send()
+
+    square_ref[...] = jnp.sum(sums_in[...], axis=0)
+
+
+def body(slice_rows, row_owner, leaf_row, exponent, environment, ordering, sign_mask):
+    tiles = lax.axis_size("tile")
+    rows, width = slice_rows.shape
+    step = width // tiles
+    half = width // 2
+    cap = max(2, (3 * rows + 2 * tiles - 1) // (2 * tiles))
+    cap = (cap + 15) // 16 * 16
+    slots = tiles * cap
+    count = 2 * tiles
+    vmem, dma = pltpu.VMEM, pltpu.SemaphoreType.DMA
+    block, square = pl.pallas_call(
+        functools.partial(kernel, tiles, cap),
+        out_shape=(jax.ShapeDtypeStruct((step, half), F32), jax.ShapeDtypeStruct((8, 128), F32)),
+        in_specs=[pl.BlockSpec(memory_space=vmem)] * 7,
+        out_specs=(pl.BlockSpec(memory_space=vmem), pl.BlockSpec(memory_space=vmem)),
+        scratch_shapes=[
+            vmem((slots, width), F32), vmem((tiles, 1, slots), F32),
+            vmem((slots, width), F32), vmem((tiles, 1, slots), F32),
+            vmem((width, width), F32), vmem((width, width), BF16), vmem((width, width), BF16),
+            vmem((width, width), BF16), vmem((width, width), BF16),
+            vmem((width, width), F32), vmem((width, width), F32), vmem((width, width), F32),
+            vmem((step, width), F32), vmem((half, width), F32),
+            vmem((8, 128), F32), vmem((count, 8, 128), F32),
+            dma((2, tiles)), dma((2, tiles)), dma((tiles,)), dma((tiles,)), dma((tiles,)), dma((tiles,)),
+            dma((tiles,)), dma((1,)), dma((1,)), dma((1,)),
+            dma((2, tiles // 2)), dma((tiles // 2,)), dma((tiles // 2,)), dma((count,)), dma((count,)),
+        ],
+        compiler_params=pltpu.CompilerParams(
+            collective_id=0, has_side_effects=True, vmem_limit_bytes=40 * 1024 * 1024),
+    )(slice_rows, row_owner, leaf_row.reshape(1, rows), exponent.reshape(1, rows),
+      environment, ordering, sign_mask)
+    spread = jnp.sqrt(square[0, 0] / (width * width) + 1e-06)
+    return block / spread, jnp.log(spread).reshape(1)
 
 
 def from_partner(x, axis, bit):
@@ -17,7 +371,7 @@
     )
 
 
-def body(slice_rows, row_owner, leaf_row, exponent, environment, ordering, sign_mask):
+def plain_body(slice_rows, row_owner, leaf_row, exponent, environment, ordering, sign_mask):
     tiles = lax.axis_size("tile")
     cut_count = lax.axis_size("cuts")
     width = slice_rows.shape[1]
@@ -64,8 +418,10 @@
 
 
 def solution(mesh):
+    tiles, cuts = mesh.shape["tile"], mesh.shape["cuts"]
+    fits = cuts == 2 and 4 <= tiles <= 16
     return jax.shard_map(
-        body,
+        body if fits else plain_body,
         mesh=mesh,
         in_specs=(
             P(("groups", "tile", "cuts"), None),

time: 159 us -> 85.7 us (0.54)
  waiting for transfers between devices: 111 us -> 0 us
  Pallas kernels: 0 us -> 78.1 us
  starting transfers between devices: 15.5 us -> 0 us
  matrix products: 14.7 us -> 0 us
  other arithmetic: 9.06 us -> 0.64 us
    ppermute x4 -> x0, waiting for transfers between devices: 90.2 us -> none  [from_partner(): lax.ppermute(x, axis, [(i, i ^ 1 << bit) for i in range(lax.axis_size(axi...]
    pallas_call x0 -> x1, Pallas kernels: none -> 78.1 us  [body(): pl.pallas_call(functools.partial(kernel, tiles, cap), out_shape=(jax.Shap...]
    all_to_all x2 -> x0, waiting for transfers between devices: 21.2 us -> none  [the longest x1 17.7 us: body(): lax.all_to_all(outgoing, 'tile', split_axis=0, concat_axis=0, tiled=True)]
    dot_general x5 -> x0, matrix products: 14.7 us -> none  [multiply(): jnp.dot(left_factor, right_factor, precision=lax.Precision.HIGHEST, prefe...]
    all_to_all x2 -> x0, starting transfers between devices: 11.1 us -> none  [the longest x1 7.38 us: body(): lax.all_to_all(outgoing_rows, 'tile', split_axis=0, concat_axis=0, tiled=...]
    ppermute x4 -> x0, starting transfers between devices: 4.44 us -> none  [from_partner(): lax.ppermute(x, axis, [(i, i ^ 1 << bit) for i in range(lax.axis_size(axi...]
    scatter-add x1 -> x0, other arithmetic: 3.26 us -> none  [body(): jnp.zeros((width, width), jnp.float32).at[arrived_rows].add(arrived)]
    scatter x1 -> x0, other arithmetic: 2.9 us -> none  [body(): jnp.zeros((tiles * capacity, width), jnp.float32).at[placed].set(scaled)]
  transfers between devices with their start and end apart: 6 -> 0, of which waited for: 6 -> 0; matrix products, arithmetic and copies ran while one was open for 3% -> 0% of each run, Pallas kernels for 0% -> 0%
where the time goes in v1:
time: 85.7 us; the launch traced here: 85.5 us
  Pallas kernels  78.1 us (91%)
  local copies, waits for them, and re-layouts  4.16 us (5%)
  between operations  2.53 us (3%)
    pallas_call x1, Pallas kernels, body(): pl.pallas_call(functools.partial(kernel, tiles, cap), out_shape=(jax.Shap...  78.1 us
    unnamed x15, local copies, waits for them, and re-layouts  3.65 us

profile of v1, /device:TPU:0, one launch (start us, length us, event | category | flops | bytes accessed | tf_op | source)
XLA Modules:
  0.0 85.5 jit_solution(16882284484607557988)
XLA Ops:
  0.6 0.0 copy-start.6
  0.6 0.7 copy-done.6
  1.3 0.0 copy-start.2
  1.3 0.0 copy-start.3
  1.3 0.0 copy-start.4
  1.3 0.0 copy-start.5
  1.3 0.1 copy.9.owner_ref
  1.5 0.5 copy-done.2
  2.0 0.0 copy-done.3
  2.0 0.0 copy-done.4
  2.0 0.0 copy-done.5
  2.0 0.0 copy-start
  2.0 1.2 %copy-done = f32[512,512]{1,0:T(8,128)S(1)} copy-done((f32[512,512]{1,0:T(8,128)S(1)}, f32[512,512]{1,0:T(8,128)}, u32[]{:S(2)}) %copy-start) | copy-done | bytes 1048600
  3.3 0.0 copy-start.1
  3.3 1.0 %copy-done.1 = f32[256,512]{1,0:T(8,128)S(1)} copy-done((f32[256,512]{1,0:T(8,128)S(1)}, f32[256,512]{1,0:T(8,128)}, u32[]{:S(2)}) %copy-start.1) | copy-done | bytes 524312
  4.3 78.1 %shard_map.86 = (f32[64,256]{1,0:T(8,128)S(1)}, f32[8,128]{1,0:T(8,128)S(1)}) custom-call(f32[256,512]{1,0:T(8,128)S(1)} %copy-done.1, s32[256,1]{1,0:T(8,128)S(1)} %copy.9.owner_ref, s32[1,256]{1,0:T(1,128)S(1)} %bitcast.4, s32[1,256]{1,0:T(1,128)S(1)} %bitcast.5, f32[512,512]{1,0:T(8,128)S(1)} %copy-done, s32[1,512]{1,0:T(1,128)S(1)} %copy-done.2, ...), custom_call_target="tpu_custom_call" | custom-call | tf_op jit(solution)/shard_map/pallas_call | solution.py:336
  82.5 0.5 slice.3
  83.7 0.6 broadcast_divide_fusion
Async XLA Ops:
  0.6 0.7 copy-start.6
  1.3 0.7 copy-start.2
  1.3 0.7 copy-start.3
  1.3 0.7 copy-start.4
  1.3 0.7 copy-start.5
  2.0 1.2 %copy-start = (f32[512,512]{1,0:T(8,128)S(1)}, f32[512,512]{1,0:T(8,128)}, u32[]{:S(2)}) copy-start(f32[512,512]{1,0:T(8,128)} %env_ref.1) | copy-start | bytes 3145732
  3.3 1.0 %copy-start.1 = (f32[256,512]{1,0:T(8,128)S(1)}, f32[256,512]{1,0:T(8,128)}, u32[]{:S(2)}) copy-start(f32[256,512]{1,0:T(8,128)} %rows_ref.1) | copy-start | bytes 1572868

commit v2 on v1

--- a/solution.py
+++ b/solution.py
@@ -26,26 +26,38 @@
     return (dot(left[0], right[1], dims) + dot(left[1], right[0], dims)) + dot(left[0], right[0], dims)
 
 
-def kernel(tiles, cap,
+def kernel(tiles, cap, parts,
            rows_ref, owner_ref, leaf_row_ref, exponent_ref, env_ref, ordering_ref, sign_ref,
            block_ref, square_ref,
-           out_rows, out_ids, in_rows, in_ids, own, own_high, own_low, chain_high, chain_low,
-           pair_in, chain_in, chain_out, p_in, q_in, sums_out, sums_in,
-           route_send, route_recv, pair_send, pair_recv, chain_send, chain_recv,
+           rows_in, env_in, out_rows, out_ids, in_rows, in_ids, bond_out, bond_in, env_out, env_far,
+           own, far, own_high, own_low, chain_high, chain_low,
+           chain_in, chain_out, p_in, q_in, sums_out, sums_in,
+           load, route_send, route_recv, far_send, far_recv, chain_send, chain_recv,
            p_send, p_recv, pass_send, pass_recv, q_send, q_recv, half_send, sum_send, sum_recv):
     group, me, cut = lax.axis_index("groups"), lax.axis_index("tile"), lax.axis_index("cuts")
+    load_env = pltpu.make_async_copy(env_ref, env_in, load.at[0])
+    load_rows = pltpu.make_async_copy(rows_ref, rows_in, load.at[1])
+    load_env.start()
+    load_rows.start()
     rows, width = rows_ref.shape
     step = width // tiles
-    half = tiles // 2
+    pairs = tiles // 2
+    bits = pairs * parts
+    bit_rows = step // parts
     slots = tiles * cap
     count = 2 * tiles
     ident = me * 2 + cut
     place = jnp.where(cut == 0, me, tiles - 1 - me)
     way = 1 - 2 * cut
     last = place == tiles - 1
+    host = lax.rem(place, 2) == 1
+    pair_me = me // 2
 
     def chunk(ref, k):
         return ref.at[pl.ds(pl.multiple_of(k * step, 8), step)]
+
+    def part(ref, i):
+        return ref.at[pl.ds(pl.multiple_of(i * bit_rows, 8), bit_rows)]
 
     def remote(src, dst, send, recv, tile, other):
         return pltpu.make_async_remote_copy(
@@ -59,11 +71,35 @@
         peer = lax.rem(ident + d, count)
         pl.semaphore_signal(barrier, inc=1, device_id=(group, peer // 2, lax.rem(peer, 2)), device_id_type=MESH)
 
-    square = 128 * ((rows + 127) // 128)
+    bond_out[0:1] = ordering_ref[...]
+    bond_out[1:2] = sign_ref[...]
+    load_env.wait()
+
+    @pl.when(cut == 0)
+    def _():
+        env_out[...] = env_in[...]
+
+    @pl.when(cut == 1)
+    def _():
+        env_out[...] = env_in[...].T
+
+    def to_host():
+        to = lax.rem(me + way + tiles, tiles)
+        return (remote(bond_out, bond_in, far_send.at[0], far_recv.at[0], to, cut),
+                remote(env_out, env_far, far_send.at[1], far_recv.at[1], to, cut))
+
+    pl.semaphore_wait(barrier, count - 1)
+
+    @pl.when(jnp.logical_not(host))
+    def _():
+        for copy in to_host():
+            copy.start()
+
+    load_rows.wait()
     level = exponent_ref[...]
     factor = jnp.where(level == -1, 0.5, jnp.where(level == 1, 2.0, 1.0)).astype(F32)
     factor = jnp.broadcast_to(factor, (128, rows)).T[:, 0:1]
-    scaled = rows_ref[...] * factor
+    scaled = rows_in[...] * factor
     owner = owner_ref[...]
     hits = (owner == lax.broadcasted_iota(jnp.int32, (rows, 128), 1)).astype(F32)
     earlier = (lax.broadcasted_iota(jnp.int32, (rows, rows), 1)
@@ -78,7 +114,7 @@
     rest = scaled - high.astype(F32)
     middle = rest.astype(BF16)
     low = (rest - middle.astype(F32)).astype(BF16)
-    out_rows[...] = (dot(pick, low) + dot(pick, middle)) + dot(pick, high)
+    out_rows[...] = ((dot(pick, low) + dot(pick, middle)) + dot(pick, high)).reshape(tiles, cap, width)
     seat = (slot == me * cap + position).astype(F32).astype(BF16)
     named = jnp.where(lax.broadcasted_iota(jnp.int32, (tiles, rows), 0) == owner,
                       leaf_row_ref[...] + 1, 0).astype(F32)
@@ -87,59 +123,75 @@
     for t in range(tiles):
         out_ids[t] = ids[t:t + 1, :]
 
-    pl.semaphore_wait(barrier, count - 1)
-
-    def slots_of(ref, t):
-        return ref.at[pl.ds(pl.multiple_of(t * cap, 8), cap)]
-
-    def route(to, source):
-        return (remote(slots_of(out_rows, to), slots_of(in_rows, source), route_send.at[0, to],
+    def slots_of(source):
+        return pl.ds(pl.multiple_of(source * cap, 8), cap)
+
+    def route(pair, source):
+        both = pl.ds(2 * pair, 2)
+        to = 2 * pair + 1 - cut
+        return (remote(out_rows.at[both], in_rows.at[:, slots_of(source)], route_send.at[0, pair],
                        route_recv.at[0, source], to, cut),
-                remote(out_ids.at[to], in_ids.at[source], route_send.at[1, to],
+                remote(out_ids.at[both], in_ids.at[:, source], route_send.at[1, pair],
                        route_recv.at[1, source], to, cut))
 
-    @pl.loop(1, tiles)
+    @pl.loop(1, pairs)
     def _(d):
-        for copy in route(lax.rem(me + d, tiles), me):
+        for copy in route(lax.rem(pair_me + d, pairs), me):
             copy.start()
 
-    mine = pl.ds(pl.multiple_of(me * cap, 8), cap)
-    in_rows[mine] = out_rows[mine]
-    in_ids[me] = out_ids[me]
-    bond = jnp.where(lax.broadcasted_iota(jnp.int32, (width, width), 0) == ordering_ref[...],
-                     (1 - 2 * sign_ref[...]).astype(F32), 0.0)
-
-    @pl.when(cut == 0)
-    def _():
-        own[...] = bond.T
-        own_high[...], own_low[...] = halves(env_ref[...])
-
-    @pl.when(cut == 1)
-    def _():
-        own[...] = bond
-        own_high[...], own_low[...] = halves(env_ref[...].T)
-
-    @pl.loop(1, tiles)
-    def _(d):
-        source = lax.rem(me + d, tiles)
-        for copy in route(source, source):
-            copy.wait_recv()
-
-    wanted = jnp.sum(in_ids[...], axis=0).astype(jnp.int32) - 1
-    spread_out = (lax.broadcasted_iota(jnp.int32, (width, slots), 0) == wanted).astype(F32).astype(BF16)
-    in_high, in_low = halves(in_rows[...])
-    collected = halves(dot(spread_out, in_low) + dot(spread_out, in_high))
-
-    @pl.when(cut == 0)
-    def _():
-        own[...] += dot3(collected, (own_high[...], own_low[...]))
-
-    @pl.when(cut == 1)
-    def _():
-        own[...] += dot3((own_high[...], own_low[...]), collected, NT)
-
-    def pair(k):
-        return remote(chunk(own, k), chunk(pair_in, k), pair_send.at[k], pair_recv.at[k], me + way, cut)
+    @pl.when(jnp.logical_not(host))
+    def _():
+        for copy in route(pair_me, me):
+            copy.start()
+
+    def bond_of(order, sign):
+        return jnp.where(lax.broadcasted_iota(jnp.int32, (width, width), 0) == order,
+                         (1 - 2 * sign).astype(F32), 0.0)
+
+    @pl.when(host)
+    def _():
+        for c in range(2):
+            in_rows[c, slots_of(me)] = out_rows[2 * pair_me + c]
+            in_ids[c, me] = out_ids[2 * pair_me + c]
+        to_host()[0].wait_recv()
+
+        @pl.when(cut == 0)
+        def _():
+            own[...] = bond_of(bond_out[0:1], bond_out[1:2]).T
+            far[...] = bond_of(bond_in[0:1], bond_in[1:2]).T
+
+        @pl.when(cut == 1)
+        def _():
+            own[...] = bond_of(bond_out[0:1], bond_out[1:2])
+            far[...] = bond_of(bond_in[0:1], bond_in[1:2])
+
+        own_high[...], own_low[...] = halves(env_out[...])
+        to_host()[1].wait_recv()
+        chain_high[...], chain_low[...] = halves(env_far[...])
+
+        @pl.loop(1, tiles)
+        def _(d):
+            source = lax.rem(me + d, tiles)
+            for copy in route(pair_me, source):
+                copy.wait_recv()
+
+        def collected(c):
+            wanted = jnp.sum(in_ids[c], axis=0).astype(jnp.int32) - 1
+            spread_out = (lax.broadcasted_iota(jnp.int32, (width, slots), 0) == wanted).astype(F32).astype(BF16)
+            in_high, in_low = halves(in_rows[c])
+            return halves(dot(spread_out, in_low) + dot(spread_out, in_high))
+
+        @pl.when(cut == 0)
+        def _():
+            own[...] += dot3(collected(1), (own_high[...], own_low[...]))
+            far[...] += dot3(collected(0), (chain_high[...], chain_low[...]))
+
+        @pl.when(cut == 1)
+        def _():
+            own[...] += dot3((own_high[...], own_low[...]), collected(0), NT)
+            far[...] += dot3((chain_high[...], chain_low[...]), collected(1), NT)
+
+        own_high[...], own_low[...] = halves(own[...])
 
     def link(k):
         return remote(chunk(chain_out, k), chunk(chain_in, k), chain_send.at[k], chain_recv.at[k],
@@ -148,17 +200,16 @@
     def p_copy(k):
         return remote(chunk(chain_out, k), p_in, p_send.at[k], p_recv.at[0], k, 0)
 
-    def q_along(k):
-        return remote(chunk(q_in, k), chunk(q_in, k), q_send.at[0, k], q_recv.at[k], lax.rem(me + 2, tiles), cut)
-
-    def q_across(k):
-        return remote(chunk(q_in, k), chunk(q_in, k), q_send.at[1, k], q_recv.at[k], lax.rem(me + 1, tiles), cut)
-
-    def q_half(k):
-        return remote(chunk(chain_out, k), chunk(q_in, k), half_send.at[k], q_recv.at[k], 0, 0)
+    def q_along(i):
+        return remote(part(q_in, i), part(q_in, i), q_send.at[0, i], q_recv.at[i], lax.rem(me + 2, tiles), cut)
+
+    def q_across(i):
+        return remote(part(q_in, i), part(q_in, i), q_send.at[1, i], q_recv.at[i], lax.rem(me + 1, tiles), cut)
+
+    def q_half(i):
+        return remote(part(chain_out, i), part(q_in, i), half_send.at[i], q_recv.at[i], 0, 0)
 
     even_tile = lax.rem(me, 2) == 0
-    even_place = lax.rem(place, 2) == 0
     p_root = jnp.logical_and(last, cut == 0)
     q_root = jnp.logical_and(last, cut == 1)
 
@@ -183,52 +234,39 @@
 
         @pl.when(q_root)
         def _():
-            @pl.when(k < half)
+            @pl.when(k < pairs)
             def _():
                 chain_out[at] = value
-                q_half(k).start()
-
-            @pl.when(k >= half)
-            def _():
-                q_in[pl.ds(pl.multiple_of((k - half) * step, 8), step)] = value
-                q_along(k - half).start()
-                q_across(k - half).start()
-
-    @pl.when(even_place)
+                for i in range(parts):
+                    q_half(k * parts + i).start()
+
+            @pl.when(k >= pairs)
+            def _():
+                q_in[pl.ds(pl.multiple_of((k - pairs) * step, 8), step)] = value
+                for i in range(parts):
+                    q_along((k - pairs) * parts + i).start()
+                    q_across((k - pairs) * parts + i).start()
+
+    @pl.when(place == 1)
     def _():
         @pl.loop(0, tiles)
         def _(k):
-            pair(k).start()
-
-    @pl.when(jnp.logical_not(even_place))
-    def _():
-        own_high[...], own_low[...] = halves(own[...])
+            at = pl.ds(pl.multiple_of(k * step, 8), step)
+            emit(k, dot3(halves(far[at]), (own_high[...], own_low[...])))
+
+    @pl.when(jnp.logical_and(host, place > 1))
+    def _():
+        chain_high[...], chain_low[...] = halves(dot3(halves(far[...]), (own_high[...], own_low[...])))
 
         @pl.loop(0, tiles)
         def _(k):
             at = pl.ds(pl.multiple_of(k * step, 8), step)
-            pair(k).wait_recv()
-            value = dot3(halves(pair_in[at]), (own_high[...], own_low[...]))
-
-            @pl.when(place == 1)
-            def _():
-                emit(k, value)
-
-            @pl.when(place > 1)
-            def _():
-                chain_high[at], chain_low[at] = halves(value)
-
-        @pl.when(place > 1)
-        def _():
-            @pl.loop(0, tiles)
-            def _(k):
-                at = pl.ds(pl.multiple_of(k * step, 8), step)
-                link(k).wait_recv()
-                emit(k, dot3(halves(chain_in[at]), (chain_high[...], chain_low[...])))
+            link(k).wait_recv()
+            emit(k, dot3(halves(chain_in[at]), (chain_high[...], chain_low[...])))
 
     @pl.when(jnp.logical_not(q_root))
     def _():
-        @pl.loop(0, half)
+        @pl.loop(0, bits)
         def _(k):
             q_half(k).wait_recv()
 
@@ -271,21 +309,20 @@
 
     sums_in[ident] = total
 
-    @pl.loop(1, tiles)
+    @pl.loop(1, pairs)
     def _(d):
-        for copy in route(lax.rem(me + d, tiles), me):
+        for copy in route(lax.rem(pair_me + d, pairs), me):
             copy.wait_send()
 
-    @pl.when(even_place)
+    @pl.when(jnp.logical_not(host))
+    def _():
+        for copy in route(pair_me, me) + to_host():
+            copy.wait_send()
+
+    @pl.when(jnp.logical_and(host, jnp.logical_not(last)))
     def _():
         @pl.loop(0, tiles)
         def _(k):
-            pair(k).wait_send()
-
-    @pl.when(jnp.logical_and(jnp.logical_not(even_place), jnp.logical_not(last)))
-    def _():
-        @pl.loop(0, tiles)
-        def _(k):
             link(k).wait_send()
 
     @pl.when(p_root)
@@ -296,13 +333,13 @@
 
     @pl.when(q_root)
     def _():
-        @pl.loop(0, half)
+        @pl.loop(0, bits)
         def _(k):
             q_half(k).wait_send()
 
     @pl.when(even_tile)
     def _():
-        @pl.loop(0, half)
+        @pl.loop(0, bits)
         def _(k):
             @pl.when(me < tiles - 2)
             def _():
@@ -332,23 +369,29 @@
     cap = (cap + 15) // 16 * 16
     slots = tiles * cap
     count = 2 * tiles
+    parts = 2 if step % 32 == 0 else 1
+    bits = tiles // 2 * parts
     vmem, dma = pltpu.VMEM, pltpu.SemaphoreType.DMA
     block, square = pl.pallas_call(
-        functools.partial(kernel, tiles, cap),
+        functools.partial(kernel, tiles, cap, parts),
         out_shape=(jax.ShapeDtypeStruct((step, half), F32), jax.ShapeDtypeStruct((8, 128), F32)),
-        in_specs=[pl.BlockSpec(memory_space=vmem)] * 7,
+        in_specs=[pl.BlockSpec(memory_space=pl.ANY if i in (0, 4) else vmem) for i in range(7)],
         out_specs=(pl.BlockSpec(memory_space=vmem), pl.BlockSpec(memory_space=vmem)),
         scratch_shapes=[
-            vmem((slots, width), F32), vmem((tiles, 1, slots), F32),
-            vmem((slots, width), F32), vmem((tiles, 1, slots), F32),
-            vmem((width, width), F32), vmem((width, width), BF16), vmem((width, width), BF16),
+            vmem((rows, width), F32), vmem((width, width), F32),
+            vmem((tiles, cap, width), F32), vmem((tiles, 1, slots), F32),
+            vmem((2, slots, width), F32), vmem((2, tiles, 1, slots), F32),
+            vmem((2, width), jnp.int32), vmem((2, width), jnp.int32),
+            vmem((width, width), F32), vmem((width, width), F32),
+            vmem((width, width), F32), vmem((width, width), F32),
             vmem((width, width), BF16), vmem((width, width), BF16),
-            vmem((width, width), F32), vmem((width, width), F32), vmem((width, width), F32),
+            vmem((width, width), BF16), vmem((width, width), BF16),
+            vmem((width, width), F32), vmem((width, width), F32),
             vmem((step, width), F32), vmem((half, width), F32),
             vmem((8, 128), F32), vmem((count, 8, 128), F32),
-            dma((2, tiles)), dma((2, tiles)), dma((tiles,)), dma((tiles,)), dma((tiles,)), dma((tiles,)),
+            dma((2,)), dma((2, tiles // 2)), dma((2, tiles)), dma((2,)), dma((2,)), dma((tiles,)), dma((tiles,)),
             dma((tiles,)), dma((1,)), dma((1,)), dma((1,)),
-            dma((2, tiles // 2)), dma((tiles // 2,)), dma((tiles // 2,)), dma((count,)), dma((count,)),
+            dma((2, bits)), dma((bits,)), dma((bits,)), dma((count,)), dma((count,)),
         ],
         compiler_params=pltpu.CompilerParams(
             collective_id=0, has_side_effects=True, vmem_limit_bytes=40 * 1024 * 1024),

time: 85.7 us -> 77.6 us (0.905)
  Pallas kernels: 78.1 us -> 70 us
    pallas_call x1, Pallas kernels: 78.1 us -> 70 us  [body(): pl.pallas_call(functools.partial(kernel, tiles, cap, parts), out_shape=(j...]
where the time goes in v2:
time: 77.6 us; the launch traced here: 77.3 us
  Pallas kernels  70 us (90%)
  local copies, waits for them, and re-layouts  4.16 us (5%)
  between operations  2.53 us (3%)
    pallas_call x1, Pallas kernels, body(): pl.pallas_call(functools.partial(kernel, tiles, cap, parts), out_shape=(j...  70 us
    unnamed x15, local copies, waits for them, and re-layouts  3.65 us

profile of v2, /device:TPU:0, one launch (start us, length us, event | category | flops | bytes accessed | tf_op | source)
XLA Modules:
  0.0 77.3 jit_solution(12032894140411566268)
XLA Ops:
  0.6 0.0 copy-start.6
  0.6 0.7 copy-done.6
  1.3 0.0 copy-start.2
  1.3 0.0 copy-start.3
  1.3 0.0 copy-start.4
  1.3 0.0 copy-start.5
  1.3 0.1 copy.9.owner_ref
  1.5 0.5 copy-done.2
  2.0 0.0 copy-done.3
  2.0 0.0 copy-done.4
  2.0 0.0 copy-done.5
  2.0 0.0 copy-start
  2.0 1.2 %copy-done = f32[512,512]{1,0:T(8,128)S(1)} copy-done((f32[512,512]{1,0:T(8,128)S(1)}, f32[512,512]{1,0:T(8,128)}, u32[]{:S(2)}) %copy-start) | copy-done | bytes 1048600
  3.3 0.0 copy-start.1
  3.3 1.0 %copy-done.1 = f32[256,512]{1,0:T(8,128)S(1)} copy-done((f32[256,512]{1,0:T(8,128)S(1)}, f32[256,512]{1,0:T(8,128)}, u32[]{:S(2)}) %copy-start.1) | copy-done | bytes 524312
  4.3 70.0 %shard_map.86 = (f32[64,256]{1,0:T(8,128)S(1)}, f32[8,128]{1,0:T(8,128)S(1)}) custom-call(f32[256,512]{1,0:T(8,128)S(1)} %copy-done.1, s32[256,1]{1,0:T(8,128)S(1)} %copy.9.owner_ref, s32[1,256]{1,0:T(1,128)S(1)} %bitcast.4, s32[1,256]{1,0:T(1,128)S(1)} %bitcast.5, f32[512,512]{1,0:T(8,128)S(1)} %copy-done, s32[1,512]{1,0:T(1,128)S(1)} %copy-done.2, ...), custom_call_target="tpu_custom_call" | custom-call | tf_op jit(solution)/shard_map/pallas_call | solution.py:375
  74.3 0.5 slice.3
  75.5 0.6 broadcast_divide_fusion
Async XLA Ops:
  0.6 0.7 copy-start.6
  1.3 0.7 copy-start.2
  1.3 0.7 copy-start.3
  1.3 0.7 copy-start.4
  1.3 0.7 copy-start.5
  2.0 1.2 %copy-start = (f32[512,512]{1,0:T(8,128)S(1)}, f32[512,512]{1,0:T(8,128)}, u32[]{:S(2)}) copy-start(f32[512,512]{1,0:T(8,128)} %env_ref.1) | copy-start | bytes 3145732
  3.3 1.0 %copy-start.1 = (f32[256,512]{1,0:T(8,128)S(1)}, f32[256,512]{1,0:T(8,128)}, u32[]{:S(2)}) copy-start(f32[256,512]{1,0:T(8,128)} %rows_ref.1) | copy-start | bytes 1572868

commit v3 on v2

--- a/solution.py
+++ b/solution.py
@@ -31,6 +31,7 @@
            block_ref, square_ref,
            rows_in, env_in, out_rows, out_ids, in_rows, in_ids, bond_out, bond_in, env_out, env_far,
            own, far, own_high, own_low, chain_high, chain_low,
+           turned_high, turned_low, seated,
            chain_in, chain_out, p_in, q_in, sums_out, sums_in,
            load, route_send, route_recv, far_send, far_recv, chain_send, chain_recv,
            p_send, p_recv, pass_send, pass_recv, q_send, q_recv, half_send, sum_send, sum_recv):
@@ -45,6 +46,7 @@
     bits = pairs * parts
     bit_rows = step // parts
     slots = tiles * cap
+    lane = 128 // 2
     count = 2 * tiles
     ident = me * 2 + cut
     place = jnp.where(cut == 0, me, tiles - 1 - me)
@@ -115,7 +117,8 @@
     middle = rest.astype(BF16)
     low = (rest - middle.astype(F32)).astype(BF16)
     out_rows[...] = ((dot(pick, low) + dot(pick, middle)) + dot(pick, high)).reshape(tiles, cap, width)
-    seat = (slot == me * cap + position).astype(F32).astype(BF16)
+    seat = (lax.broadcasted_iota(jnp.int32, (128, rows), 0) == lax.rem(me, 2) * lane + position)
+    seat = seat.astype(F32).astype(BF16)
     named = jnp.where(lax.broadcasted_iota(jnp.int32, (tiles, rows), 0) == owner,
                       leaf_row_ref[...] + 1, 0).astype(F32)
     named_high, named_low = halves(named)
@@ -124,7 +127,7 @@
         out_ids[t] = ids[t:t + 1, :]
 
     def slots_of(source):
-        return pl.ds(pl.multiple_of(source * cap, 8), cap)
+        return pl.ds(pl.multiple_of(source * lane, 8), cap)
 
     def route(pair, source):
         both = pl.ds(2 * pair, 2)
@@ -165,31 +168,51 @@
             own[...] = bond_of(bond_out[0:1], bond_out[1:2])
             far[...] = bond_of(bond_in[0:1], bond_in[1:2])
 
+        for t in range(tiles):
+            if cap < lane:
+                in_rows[:, t * lane + cap:(t + 1) * lane] = jnp.zeros((2, lane - cap, width), F32)
         own_high[...], own_low[...] = halves(env_out[...])
         to_host()[1].wait_recv()
         chain_high[...], chain_low[...] = halves(env_far[...])
 
-        @pl.loop(1, tiles)
+        @pl.loop(0, pairs)
         def _(d):
-            source = lax.rem(me + d, tiles)
-            for copy in route(pair_me, source):
-                copy.wait_recv()
-
-        def collected(c):
-            wanted = jnp.sum(in_ids[c], axis=0).astype(jnp.int32) - 1
-            spread_out = (lax.broadcasted_iota(jnp.int32, (width, slots), 0) == wanted).astype(F32).astype(BF16)
-            in_high, in_low = halves(in_rows[c])
-            return halves(dot(spread_out, in_low) + dot(spread_out, in_high))
+            pair = lax.rem(jnp.where(pair_me < pairs // 2, pair_me + d, pair_me + pairs - d), pairs)
+            for c in range(2):
+                @pl.when(2 * pair + c != me)
+                def _():
+                    for copy in route(pair_me, 2 * pair + c):
+                        copy.wait_recv()
+            lanes = pl.ds(pl.multiple_of(pair * 128, 128), 128)
+
+            for c in range(2):
+                wanted = (in_ids[c, 2 * pair] + in_ids[c, 2 * pair + 1]).astype(jnp.int32) - 1
+                seated[c, :, lanes] = (
+                    lax.broadcasted_iota(jnp.int32, (width, 128), 0) == wanted).astype(F32).astype(BF16)
+
+            def turn(c, environment):
+                arrived = halves(in_rows[c, lanes])
+
+                @pl.when(cut == 0)
+                def _():
+                    turned_high[c, lanes], turned_low[c, lanes] = halves(dot3(arrived, environment))
+
+                @pl.when(cut == 1)
+                def _():
+                    turned_high[c, :, lanes], turned_low[c, :, lanes] = halves(dot3(environment, arrived, NT))
+
+            turn(1 - cut, (own_high[...], own_low[...]))
+            turn(cut, (chain_high[...], chain_low[...]))
 
         @pl.when(cut == 0)
         def _():
-            own[...] += dot3(collected(1), (own_high[...], own_low[...]))
-            far[...] += dot3(collected(0), (chain_high[...], chain_low[...]))
+            own[...] += dot(seated[1], turned_low[1]) + dot(seated[1], turned_high[1])
+            far[...] += dot(seated[0], turned_low[0]) + dot(seated[0], turned_high[0])
 
         @pl.when(cut == 1)
         def _():
-            own[...] += dot3((own_high[...], own_low[...]), collected(0), NT)
-            far[...] += dot3((chain_high[...], chain_low[...]), collected(1), NT)
+            own[...] += dot(turned_low[0], seated[0], NT) + dot(turned_high[0], seated[0], NT)
+            far[...] += dot(turned_low[1], seated[1], NT) + dot(turned_high[1], seated[1], NT)
 
         own_high[...], own_low[...] = halves(own[...])
 
@@ -367,7 +390,9 @@
     half = width // 2
     cap = max(2, (3 * rows + 2 * tiles - 1) // (2 * tiles))
     cap = (cap + 15) // 16 * 16
-    slots = tiles * cap
+    if lax.axis_size("cuts") != 2 or cap > 64 or width != tiles * 64:
+        return plain_body(slice_rows, row_owner, leaf_row, exponent, environment, ordering, sign_mask)
+    places = tiles * 64
     count = 2 * tiles
     parts = 2 if step % 32 == 0 else 1
     bits = tiles // 2 * parts
@@ -375,17 +400,19 @@
     block, square = pl.pallas_call(
         functools.partial(kernel, tiles, cap, parts),
         out_shape=(jax.ShapeDtypeStruct((step, half), F32), jax.ShapeDtypeStruct((8, 128), F32)),
-        in_specs=[pl.BlockSpec(memory_space=pl.ANY if i in (0, 4) else vmem) for i in range(7)],
+        in_specs=[pl.BlockSpec(memory_space=pltpu.HBM if i in (0, 4) else vmem) for i in range(7)],
         out_specs=(pl.BlockSpec(memory_space=vmem), pl.BlockSpec(memory_space=vmem)),
         scratch_shapes=[
             vmem((rows, width), F32), vmem((width, width), F32),
-            vmem((tiles, cap, width), F32), vmem((tiles, 1, slots), F32),
-            vmem((2, slots, width), F32), vmem((2, tiles, 1, slots), F32),
+            vmem((tiles, cap, width), F32), vmem((tiles, 1, 128), F32),
+            vmem((2, places, width), F32), vmem((2, tiles, 1, 128), F32),
             vmem((2, width), jnp.int32), vmem((2, width), jnp.int32),
             vmem((width, width), F32), vmem((width, width), F32),
             vmem((width, width), F32), vmem((width, width), F32),
             vmem((width, width), BF16), vmem((width, width), BF16),
             vmem((width, width), BF16), vmem((width, width), BF16),
+            vmem((2, max(width, places), max(width, places)), BF16),
+            vmem((2, max(width, places), max(width, places)), BF16), vmem((2, width, places), BF16),
             vmem((width, width), F32), vmem((width, width), F32),
             vmem((step, width), F32), vmem((half, width), F32),
             vmem((8, 128), F32), vmem((count, 8, 128), F32),
@@ -461,10 +488,8 @@
 
 
 def solution(mesh):
-    tiles, cuts = mesh.shape["tile"], mesh.shape["cuts"]
-    fits = cuts == 2 and 4 <= tiles <= 16
     return jax.shard_map(
-        body if fits else plain_body,
+        body,
         mesh=mesh,
         in_specs=(
             P(("groups", "tile", "cuts"), None),

time: 77.6 us -> 80.8 us (1.041)
  Pallas kernels: 70 us -> 73.2 us
    pallas_call x1, Pallas kernels: 70 us -> 73.2 us  [body(): pl.pallas_call(functools.partial(kernel, tiles, cap, parts), out_shape=(j...]
where the time goes in v3:
time: 80.8 us; the launch traced here: 80.5 us
  Pallas kernels  73.2 us (91%)
  local copies, waits for them, and re-layouts  4.16 us (5%)
  between operations  2.53 us (3%)
    pallas_call x1, Pallas kernels, body(): pl.pallas_call(functools.partial(kernel, tiles, cap, parts), out_shape=(j...  73.2 us
    unnamed x15, local copies, waits for them, and re-layouts  3.65 us

profile of v3, /device:TPU:0, one launch (start us, length us, event | category | flops | bytes accessed | tf_op | source)
XLA Modules:
  0.0 80.5 jit_solution(10485309028363201550)
XLA Ops:
  0.6 0.0 copy-start.6
  0.6 0.7 copy-done.6
  1.3 0.0 copy-start.2
  1.3 0.0 copy-start.3
  1.3 0.0 copy-start.4
  1.3 0.0 copy-start.5
  1.3 0.1 copy.9.owner_ref
  1.5 0.5 copy-done.2
  2.0 0.0 copy-done.3
  2.0 0.0 copy-done.4
  2.0 0.0 copy-done.5
  2.0 0.0 copy-start
  2.0 1.2 %copy-done = f32[512,512]{1,0:T(8,128)S(1)} copy-done((f32[512,512]{1,0:T(8,128)S(1)}, f32[512,512]{1,0:T(8,128)}, u32[]{:S(2)}) %copy-start) | copy-done | bytes 1048600
  3.3 0.0 copy-start.1
  3.3 1.0 %copy-done.1 = f32[256,512]{1,0:T(8,128)S(1)} copy-done((f32[256,512]{1,0:T(8,128)S(1)}, f32[256,512]{1,0:T(8,128)}, u32[]{:S(2)}) %copy-start.1) | copy-done | bytes 524312
  4.3 73.2 %shard_map.86 = (f32[64,256]{1,0:T(8,128)S(1)}, f32[8,128]{1,0:T(8,128)S(1)}) custom-call(f32[256,512]{1,0:T(8,128)S(1)} %copy-done.1, s32[256,1]{1,0:T(8,128)S(1)} %copy.9.owner_ref, s32[1,256]{1,0:T(1,128)S(1)} %bitcast.4, s32[1,256]{1,0:T(1,128)S(1)} %bitcast.5, f32[512,512]{1,0:T(8,128)S(1)} %copy-done, s32[1,512]{1,0:T(1,128)S(1)} %copy-done.2, ...), custom_call_target="tpu_custom_call" | custom-call | tf_op jit(solution)/shard_map/pallas_call | solution.py:400
  77.5 0.5 slice.3
  78.7 0.6 broadcast_divide_fusion
Async XLA Ops:
  0.6 0.7 copy-start.6
  1.3 0.7 copy-start.2
  1.3 0.7 copy-start.3
  1.3 0.7 copy-start.4
  1.3 0.7 copy-start.5
  2.0 1.2 %copy-start = (f32[512,512]{1,0:T(8,128)S(1)}, f32[512,512]{1,0:T(8,128)}, u32[]{:S(2)}) copy-start(f32[512,512]{1,0:T(8,128)} %env_ref.1) | copy-start | bytes 3145732
  3.3 1.0 %copy-start.1 = (f32[256,512]{1,0:T(8,128)S(1)}, f32[256,512]{1,0:T(8,128)}, u32[]{:S(2)}) copy-start(f32[256,512]{1,0:T(8,128)} %rows_ref.1) | copy-start | bytes 1572868

commit v4 on v3

--- a/solution.py
+++ b/solution.py
@@ -29,11 +29,11 @@
 def kernel(tiles, cap, parts,
            rows_ref, owner_ref, leaf_row_ref, exponent_ref, env_ref, ordering_ref, sign_ref,
            block_ref, square_ref,
-           rows_in, env_in, out_rows, out_ids, in_rows, in_ids, bond_out, bond_in, env_out, env_far,
+           rows_in, env_in, out_rows, out_ids, in_rows, in_ids, bond_out, bond_in, turn_out, turn_in,
            own, far, own_high, own_low, chain_high, chain_low,
            turned_high, turned_low, seated,
            chain_in, chain_out, p_in, q_in, sums_out, sums_in,
-           load, route_send, route_recv, far_send, far_recv, chain_send, chain_recv,
+           load, route_send, route_recv, ids_send, ids_recv, bond_send, bond_recv, turn_send, turn_recv, chain_send, chain_recv,
            p_send, p_recv, pass_send, pass_recv, q_send, q_recv, half_send, sum_send, sum_recv):
     group, me, cut = lax.axis_index("groups"), lax.axis_index("tile"), lax.axis_index("cuts")
     load_env = pltpu.make_async_copy(env_ref, env_in, load.at[0])
@@ -76,26 +76,16 @@
     bond_out[0:1] = ordering_ref[...]
     bond_out[1:2] = sign_ref[...]
     load_env.wait()
-
-    @pl.when(cut == 0)
-    def _():
-        env_out[...] = env_in[...]
-
-    @pl.when(cut == 1)
-    def _():
-        env_out[...] = env_in[...].T
-
-    def to_host():
-        to = lax.rem(me + way + tiles, tiles)
-        return (remote(bond_out, bond_in, far_send.at[0], far_recv.at[0], to, cut),
-                remote(env_out, env_far, far_send.at[1], far_recv.at[1], to, cut))
+    own_high[...], own_low[...] = halves(env_in[...])
+
+    def bond_copy():
+        return remote(bond_out, bond_in, bond_send.at[0], bond_recv.at[0], lax.rem(me + way + tiles, tiles), cut)
 
     pl.semaphore_wait(barrier, count - 1)
 
     @pl.when(jnp.logical_not(host))
     def _():
-        for copy in to_host():
-            copy.start()
+        bond_copy().start()
 
     load_rows.wait()
     level = exponent_ref[...]
@@ -116,7 +106,7 @@
     rest = scaled - high.astype(F32)
     middle = rest.astype(BF16)
     low = (rest - middle.astype(F32)).astype(BF16)
-    out_rows[...] = ((dot(pick, low) + dot(pick, middle)) + dot(pick, high)).reshape(tiles, cap, width)
+    out_rows[...] = (dot(pick, low) + dot(pick, middle)) + dot(pick, high)
     seat = (lax.broadcasted_iota(jnp.int32, (128, rows), 0) == lax.rem(me, 2) * lane + position)
     seat = seat.astype(F32).astype(BF16)
     named = jnp.where(lax.broadcasted_iota(jnp.int32, (tiles, rows), 0) == owner,
@@ -129,34 +119,65 @@
     def slots_of(source):
         return pl.ds(pl.multiple_of(source * lane, 8), cap)
 
-    def route(pair, source):
-        both = pl.ds(2 * pair, 2)
-        to = 2 * pair + 1 - cut
-        return (remote(out_rows.at[both], in_rows.at[:, slots_of(source)], route_send.at[0, pair],
-                       route_recv.at[0, source], to, cut),
-                remote(out_ids.at[both], in_ids.at[:, source], route_send.at[1, pair],
-                       route_recv.at[1, source], to, cut))
+    def route(to, source):
+        return remote(out_rows.at[pl.ds(pl.multiple_of(to * cap, 8), cap)], in_rows.at[slots_of(source)],
+                      route_send.at[to], route_recv.at[source], to, cut)
+
+    def route_ids(pair, source):
+        return remote(out_ids.at[pl.ds(2 * pair, 2)], in_ids.at[:, source],
+                      ids_send.at[pair], ids_recv.at[source], 2 * pair + 1 - cut, cut)
+
+    @pl.loop(1, tiles)
+    def _(d):
+        route(lax.rem(me + d, tiles), me).start()
 
     @pl.loop(1, pairs)
     def _(d):
-        for copy in route(lax.rem(pair_me + d, pairs), me):
-            copy.start()
+        route_ids(lax.rem(pair_me + d, pairs), me).start()
 
     @pl.when(jnp.logical_not(host))
     def _():
-        for copy in route(pair_me, me):
-            copy.start()
+        route_ids(pair_me, me).start()
 
     def bond_of(order, sign):
         return jnp.where(lax.broadcasted_iota(jnp.int32, (width, width), 0) == order,
                          (1 - 2 * sign).astype(F32), 0.0)
 
+    in_rows[slots_of(me)] = out_rows[pl.ds(pl.multiple_of(me * cap, 8), cap)]
+    for t in range(tiles):
+        if cap < lane:
+            in_rows[t * lane + cap:(t + 1) * lane] = jnp.zeros((lane - cap, width), F32)
+
+    def pair_at(d):
+        return lax.rem(jnp.where(pair_me < pairs // 2, pair_me + d, pair_me + pairs - d), pairs)
+
+    def lanes_of(pair):
+        return pl.ds(pl.multiple_of(pair * 128, 128), 128)
+
+    def turn(pair):
+        for c in range(2):
+            @pl.when(2 * pair + c != me)
+            def _():
+                route(2 * pair + c, 2 * pair + c).wait_recv()
+        return dot3(halves(in_rows[lanes_of(pair)]), (own_high[...], own_low[...]))
+
+    def turn_copy(pair):
+        return remote(turn_out.at[lanes_of(pair)], turn_in.at[lanes_of(pair)],
+                      turn_send.at[pair], turn_recv.at[pair], lax.rem(me + way + tiles, tiles), cut)
+
+    @pl.when(jnp.logical_not(host))
+    def _():
+        @pl.loop(0, pairs)
+        def _(d):
+            pair = pair_at(d)
+            turn_out[lanes_of(pair)] = turn(pair)
+            turn_copy(pair).start()
+
     @pl.when(host)
     def _():
         for c in range(2):
-            in_rows[c, slots_of(me)] = out_rows[2 * pair_me + c]
             in_ids[c, me] = out_ids[2 * pair_me + c]
-        to_host()[0].wait_recv()
+        bond_copy().wait_recv()
 
         @pl.when(cut == 0)
         def _():
@@ -168,53 +189,52 @@
             own[...] = bond_of(bond_out[0:1], bond_out[1:2])
             far[...] = bond_of(bond_in[0:1], bond_in[1:2])
 
-        for t in range(tiles):
-            if cap < lane:
-                in_rows[:, t * lane + cap:(t + 1) * lane] = jnp.zeros((2, lane - cap, width), F32)
-        own_high[...], own_low[...] = halves(env_out[...])
-        to_host()[1].wait_recv()
-        chain_high[...], chain_low[...] = halves(env_far[...])
+        def keep(c, pair, value):
+            lanes = lanes_of(pair)
+
+            @pl.when(cut == 0)
+            def _():
+                turned_high[c, lanes], turned_low[c, lanes] = halves(value)
+
+            @pl.when(cut == 1)
+            def _():
+                turned_high[c, :, lanes], turned_low[c, :, lanes] = halves(value.T)
+
+        def keep_far(pair):
+            turn_copy(pair).wait_recv()
+            keep(0, pair, turn_in[lanes_of(pair)])
 
         @pl.loop(0, pairs)
         def _(d):
-            pair = lax.rem(jnp.where(pair_me < pairs // 2, pair_me + d, pair_me + pairs - d), pairs)
+            pair = pair_at(d)
+            keep(1, pair, turn(pair))
             for c in range(2):
                 @pl.when(2 * pair + c != me)
                 def _():
-                    for copy in route(pair_me, 2 * pair + c):
-                        copy.wait_recv()
-            lanes = pl.ds(pl.multiple_of(pair * 128, 128), 128)
-
+                    route_ids(pair_me, 2 * pair + c).wait_recv()
             for c in range(2):
-                wanted = (in_ids[c, 2 * pair] + in_ids[c, 2 * pair + 1]).astype(jnp.int32) - 1
-                seated[c, :, lanes] = (
+                named_there = jnp.where(cut == 0, c, 1 - c)
+                wanted = (in_ids[named_there, 2 * pair] + in_ids[named_there, 2 * pair + 1]).astype(jnp.int32) - 1
+                seated[c, :, lanes_of(pair)] = (
                     lax.broadcasted_iota(jnp.int32, (width, 128), 0) == wanted).astype(F32).astype(BF16)
 
-            def turn(c, environment):
-                arrived = halves(in_rows[c, lanes])
-
-                @pl.when(cut == 0)
-                def _():
-                    turned_high[c, lanes], turned_low[c, lanes] = halves(dot3(arrived, environment))
-
-                @pl.when(cut == 1)
-                def _():
-                    turned_high[c, :, lanes], turned_low[c, :, lanes] = halves(dot3(environment, arrived, NT))
-
-            turn(1 - cut, (own_high[...], own_low[...]))
-            turn(cut, (chain_high[...], chain_low[...]))
-
-        @pl.when(cut == 0)
-        def _():
-            own[...] += dot(seated[1], turned_low[1]) + dot(seated[1], turned_high[1])
-            far[...] += dot(seated[0], turned_low[0]) + dot(seated[0], turned_high[0])
-
-        @pl.when(cut == 1)
-        def _():
-            own[...] += dot(turned_low[0], seated[0], NT) + dot(turned_high[0], seated[0], NT)
-            far[...] += dot(turned_low[1], seated[1], NT) + dot(turned_high[1], seated[1], NT)
-
+            @pl.when(d > 0)
+            def _():
+                keep_far(pair_at(d - 1))
+
+        def leaf(ref, c):
+            @pl.when(cut == 0)
+            def _():
+                ref[...] += dot(seated[c], turned_low[c]) + dot(seated[c], turned_high[c])
+
+            @pl.when(cut == 1)
+            def _():
+                ref[...] += dot(turned_low[c], seated[c], NT) + dot(turned_high[c], seated[c], NT)
+
+        leaf(own, 1)
         own_high[...], own_low[...] = halves(own[...])
+        keep_far(pair_at(pairs - 1))
+        leaf(far, 0)
 
     def link(k):
         return remote(chunk(chain_out, k), chunk(chain_in, k), chain_send.at[k], chain_recv.at[k],
@@ -332,15 +352,22 @@
 
     sums_in[ident] = total
 
+    @pl.loop(1, tiles)
+    def _(d):
+        route(lax.rem(me + d, tiles), me).wait_send()
+
     @pl.loop(1, pairs)
     def _(d):
-        for copy in route(lax.rem(pair_me + d, pairs), me):
-            copy.wait_send()
+        route_ids(lax.rem(pair_me + d, pairs), me).wait_send()
 
     @pl.when(jnp.logical_not(host))
     def _():
-        for copy in route(pair_me, me) + to_host():
-            copy.wait_send()
+        route_ids(pair_me, me).wait_send()
+        bond_copy().wait_send()
+
+        @pl.loop(0, pairs)
+        def _(pair):
+            turn_copy(pair).wait_send()
 
     @pl.when(jnp.logical_and(host, jnp.logical_not(last)))
     def _():
@@ -404,10 +431,10 @@
         out_specs=(pl.BlockSpec(memory_space=vmem), pl.BlockSpec(memory_space=vmem)),
         scratch_shapes=[
             vmem((rows, width), F32), vmem((width, width), F32),
-            vmem((tiles, cap, width), F32), vmem((tiles, 1, 128), F32),
-            vmem((2, places, width), F32), vmem((2, tiles, 1, 128), F32),
+            vmem((tiles * cap, width), F32), vmem((tiles, 1, 128), F32),
+            vmem((places, width), F32), vmem((2, tiles, 1, 128), F32),
             vmem((2, width), jnp.int32), vmem((2, width), jnp.int32),
-            vmem((width, width), F32), vmem((width, width), F32),
+            vmem((places, width), F32), vmem((places, width), F32),
             vmem((width, width), F32), vmem((width, width), F32),
             vmem((width, width), BF16), vmem((width, width), BF16),
             vmem((width, width), BF16), vmem((width, width), BF16),
@@ -416,12 +443,13 @@
             vmem((width, width), F32), vmem((width, width), F32),
             vmem((step, width), F32), vmem((half, width), F32),
             vmem((8, 128), F32), vmem((count, 8, 128), F32),
-            dma((2,)), dma((2, tiles // 2)), dma((2, tiles)), dma((2,)), dma((2,)), dma((tiles,)), dma((tiles,)),
+            dma((2,)), dma((tiles,)), dma((tiles,)), dma((tiles // 2,)), dma((tiles,)), dma((1,)), dma((1,)),
+            dma((tiles // 2,)), dma((tiles // 2,)), dma((tiles,)), dma((tiles,)),
             dma((tiles,)), dma((1,)), dma((1,)), dma((1,)),
             dma((2, bits)), dma((bits,)), dma((bits,)), dma((count,)), dma((count,)),
         ],
         compiler_params=pltpu.CompilerParams(
-            collective_id=0, has_side_effects=True, vmem_limit_bytes=40 * 1024 * 1024),
+            collective_id=0, has_side_effects=True, vmem_limit_bytes=60 * 1024 * 1024),
     )(slice_rows, row_owner, leaf_row.reshape(1, rows), exponent.reshape(1, rows),
       environment, ordering, sign_mask)
     spread = jnp.sqrt(square[0, 0] / (width * width) + 1e-06)

time: 80.8 us -> 84.2 us (1.042)
  Pallas kernels: 73.2 us -> 77.3 us
  local copies, waits for them, and re-layouts: 4.16 us -> 2.64 us
    pallas_call x1, Pallas kernels: 73.2 us -> 77.3 us  [body(): pl.pallas_call(functools.partial(kernel, tiles, cap, parts), out_shape=(j...]
    unnamed x15 -> x3, local copies, waits for them, and re-layouts: 3.65 us -> 1.45 us
where the time goes in v4:
time: 84.2 us; the launch traced here: 83.9 us
  Pallas kernels  77.3 us (92%)
  local copies, waits for them, and re-layouts  2.64 us (3%)
  between operations  2.51 us (3%)
  other arithmetic  1.48 us (2%)
    pallas_call x1, Pallas kernels, body(): pl.pallas_call(functools.partial(kernel, tiles, cap, parts), out_shape=(j...  77.3 us

profile of v4, /device:TPU:0, one launch (start us, length us, event | category | flops | bytes accessed | tf_op | source)
XLA Modules:
  0.0 83.9 jit_solution(18302922229506439640)
XLA Ops:
  0.6 0.0 copy-start
  0.6 0.7 copy-done
  1.3 0.8 copy.9.owner_ref
  2.1 77.3 %shard_map.86 = (f32[64,256]{1,0:T(8,128)}, f32[8,128]{1,0:T(8,128)}) custom-call(f32[256,512]{1,0:T(8,128)} %rows_ref.1, s32[256,1]{1,0:T(8,128)} %copy.9.owner_ref, s32[1,256]{1,0:T(1,128)} %bitcast.4, s32[1,256]{1,0:T(1,128)} %bitcast.5, f32[512,512]{1,0:T(8,128)} %env_ref.1, s32[1,512]{1,0:T(1,128)} %ordering_ref.1, s32[1,512]{1,0:T(1,128)} %sign_ref.1), custom_call_target="tpu_custom_call" | custom-call | tf_op jit(solution)/shard_map/pallas_call | solution.py:427
  79.4 1.2 %slice.3 = f32[1,1]{1,0:T(1,128)} slice(f32[8,128]{1,0:T(8,128)} %get-tuple-element.5), slice={[0:1], [0:1]} | slice | bytes 8 | tf_op jit(solution)/shard_map/slice | solution.py:455
  81.3 1.5 %broadcast_divide_fusion = f32[64,256]{1,0:T(8,128)} fusion(f32[64,256]{1,0:T(8,128)} %get-tuple-element.4, f32[]{:T(128)} %bitcast.2), kind=kLoop, calls=%fused_computation | loop fusion | flops 16384 | bytes 131076 | tf_op jit(solution)/shard_map/div | solution.py:456
Async XLA Ops:
  0.6 0.7 copy-start

commit v5 on v2

--- a/solution.py
+++ b/solution.py
@@ -23,7 +23,9 @@
 
 
 def dot3(left, right, dims=NN):
-    return (dot(left[0], right[1], dims) + dot(left[1], right[0], dims)) + dot(left[0], right[0], dims)
+    rows = left[0].shape[0]
+    both = dot(jnp.concatenate(left, axis=0), right[0], dims)
+    return (dot(left[0], right[1], dims) + both[rows:]) + both[:rows]
 
 
 def kernel(tiles, cap, parts,
@@ -394,7 +396,7 @@
             dma((2, bits)), dma((bits,)), dma((bits,)), dma((count,)), dma((count,)),
         ],
         compiler_params=pltpu.CompilerParams(
-            collective_id=0, has_side_effects=True, vmem_limit_bytes=40 * 1024 * 1024),
+            collective_id=0, has_side_effects=True, vmem_limit_bytes=60 * 1024 * 1024),
     )(slice_rows, row_owner, leaf_row.reshape(1, rows), exponent.reshape(1, rows),
       environment, ordering, sign_mask)
     spread = jnp.sqrt(square[0, 0] / (width * width) + 1e-06)

time: 77.6 us -> 78.5 us (1.012)
  Pallas kernels: 70 us -> 71.6 us
  local copies, waits for them, and re-layouts: 4.16 us -> 2.64 us
  other arithmetic: 0.64 us -> 1.48 us
    unnamed x15 -> x3, local copies, waits for them, and re-layouts: 3.65 us -> 1.45 us
    pallas_call x1, Pallas kernels: 70 us -> 71.6 us  [body(): pl.pallas_call(functools.partial(kernel, tiles, cap, parts), out_shape=(j...]
    div x1, other arithmetic: 0.64 us -> 1.48 us  [body(): return (block / spread, jnp.log(spread).reshape(1))]
where the time goes in v5:
time: 78.5 us; the launch traced here: 78.2 us
  Pallas kernels  71.6 us (91%)
  local copies, waits for them, and re-layouts  2.64 us (3%)
  between operations  2.51 us (3%)
  other arithmetic  1.48 us (2%)
    pallas_call x1, Pallas kernels, body(): pl.pallas_call(functools.partial(kernel, tiles, cap, parts), out_shape=(j...  71.6 us

profile of v5, /device:TPU:0, one launch (start us, length us, event | category | flops | bytes accessed | tf_op | source)
XLA Modules:
  0.0 78.2 jit_solution(15567808802504286121)
XLA Ops:
  0.6 0.0 copy-start
  0.6 0.7 copy-done
  1.3 0.8 copy.9.owner_ref
  2.1 71.6 %shard_map.86 = (f32[64,256]{1,0:T(8,128)}, f32[8,128]{1,0:T(8,128)}) custom-call(f32[256,512]{1,0:T(8,128)} %rows_ref.1, s32[256,1]{1,0:T(8,128)} %copy.9.owner_ref, s32[1,256]{1,0:T(1,128)} %bitcast.4, s32[1,256]{1,0:T(1,128)} %bitcast.5, f32[512,512]{1,0:T(8,128)} %env_ref.1, s32[1,512]{1,0:T(1,128)} %ordering_ref.1, s32[1,512]{1,0:T(1,128)} %sign_ref.1), custom_call_target="tpu_custom_call" | custom-call | tf_op jit(solution)/shard_map/pallas_call | solution.py:377
  73.7 1.2 %slice.3 = f32[1,1]{1,0:T(1,128)} slice(f32[8,128]{1,0:T(8,128)} %get-tuple-element.5), slice={[0:1], [0:1]} | slice | bytes 8 | tf_op jit(solution)/shard_map/slice | solution.py:402
  75.6 1.5 %broadcast_divide_fusion = f32[64,256]{1,0:T(8,128)} fusion(f32[64,256]{1,0:T(8,128)} %get-tuple-element.4, f32[]{:T(128)} %bitcast.2), kind=kLoop, calls=%fused_computation | loop fusion | flops 16384 | bytes 131076 | tf_op jit(solution)/shard_map/div | solution.py:403
Async XLA Ops:
  0.6 0.7 copy-start

commit v6 on v2

--- a/solution.py
+++ b/solution.py
@@ -86,13 +86,14 @@
     def to_host():
         to = lax.rem(me + way + tiles, tiles)
         return (remote(bond_out, bond_in, far_send.at[0], far_recv.at[0], to, cut),
-                remote(env_out, env_far, far_send.at[1], far_recv.at[1], to, cut))
+                remote(env_out.at[:width // 2], env_far.at[:width // 2], far_send.at[1], far_recv.at[1], to, cut),
+                remote(env_out.at[width // 2:], env_far.at[width // 2:], far_send.at[2], far_recv.at[2], to, cut))
 
     pl.semaphore_wait(barrier, count - 1)
 
     @pl.when(jnp.logical_not(host))
     def _():
-        for copy in to_host():
+        for copy in to_host()[:2]:
             copy.start()
 
     load_rows.wait()
@@ -141,7 +142,7 @@
 
     @pl.when(jnp.logical_not(host))
     def _():
-        for copy in route(pair_me, me):
+        for copy in route(pair_me, me) + to_host()[2:]:
             copy.start()
 
     def bond_of(order, sign):
@@ -166,9 +167,6 @@
             far[...] = bond_of(bond_in[0:1], bond_in[1:2])
 
         own_high[...], own_low[...] = halves(env_out[...])
-        to_host()[1].wait_recv()
-        chain_high[...], chain_low[...] = halves(env_far[...])
-
         @pl.loop(1, tiles)
         def _(d):
             source = lax.rem(me + d, tiles)
@@ -184,14 +182,24 @@
         @pl.when(cut == 0)
         def _():
             own[...] += dot3(collected(1), (own_high[...], own_low[...]))
+
+        @pl.when(cut == 1)
+        def _():
+            own[...] += dot3((own_high[...], own_low[...]), collected(0), NT)
+
+        own_high[...], own_low[...] = halves(own[...])
+        for copy in to_host()[1:]:
+            copy.wait_recv()
+        chain_high[...], chain_low[...] = halves(env_far[...])
+
+        @pl.when(cut == 0)
+        def _():
             far[...] += dot3(collected(0), (chain_high[...], chain_low[...]))
 
         @pl.when(cut == 1)
         def _():
-            own[...] += dot3((own_high[...], own_low[...]), collected(0), NT)
             far[...] += dot3((chain_high[...], chain_low[...]), collected(1), NT)
 
-        own_high[...], own_low[...] = halves(own[...])
 
     def link(k):
         return remote(chunk(chain_out, k), chunk(chain_in, k), chain_send.at[k], chain_recv.at[k],
@@ -389,7 +397,7 @@
             vmem((width, width), F32), vmem((width, width), F32),
             vmem((step, width), F32), vmem((half, width), F32),
             vmem((8, 128), F32), vmem((count, 8, 128), F32),
-            dma((2,)), dma((2, tiles // 2)), dma((2, tiles)), dma((2,)), dma((2,)), dma((tiles,)), dma((tiles,)),
+            dma((2,)), dma((2, tiles // 2)), dma((2, tiles)), dma((3,)), dma((3,)), dma((tiles,)), dma((tiles,)),
             dma((tiles,)), dma((1,)), dma((1,)), dma((1,)),
             dma((2, bits)), dma((bits,)), dma((bits,)), dma((count,)), dma((count,)),
         ],

time: 77.6 us -> 77.7 us (level)
  no operation moved by 1% of the time
where the time goes in v6:
time: 77.7 us; the launch traced here: 77.4 us
  Pallas kernels  70.1 us (90%)
  local copies, waits for them, and re-layouts  4.16 us (5%)
  between operations  2.53 us (3%)
    pallas_call x1, Pallas kernels, body(): pl.pallas_call(functools.partial(kernel, tiles, cap, parts), out_shape=(j...  70.1 us
    unnamed x15, local copies, waits for them, and re-layouts  3.65 us

profile of v6, /device:TPU:0, one launch (start us, length us, event | category | flops | bytes accessed | tf_op | source)
XLA Modules:
  0.0 77.4 jit_solution(11395996468969977057)
XLA Ops:
  0.6 0.0 copy-start.6
  0.6 0.7 copy-done.6
  1.3 0.0 copy-start.2
  1.3 0.0 copy-start.3
  1.3 0.0 copy-start.4
  1.3 0.0 copy-start.5
  1.3 0.1 copy.9.owner_ref
  1.5 0.5 copy-done.2
  2.0 0.0 copy-done.3
  2.0 0.0 copy-done.4
  2.0 0.0 copy-done.5
  2.0 0.0 copy-start
  2.0 1.2 %copy-done = f32[512,512]{1,0:T(8,128)S(1)} copy-done((f32[512,512]{1,0:T(8,128)S(1)}, f32[512,512]{1,0:T(8,128)}, u32[]{:S(2)}) %copy-start) | copy-done | bytes 1048600
  3.3 0.0 copy-start.1
  3.3 1.0 %copy-done.1 = f32[256,512]{1,0:T(8,128)S(1)} copy-done((f32[256,512]{1,0:T(8,128)S(1)}, f32[256,512]{1,0:T(8,128)}, u32[]{:S(2)}) %copy-start.1) | copy-done | bytes 524312
  4.3 70.1 %shard_map.86 = (f32[64,256]{1,0:T(8,128)S(1)}, f32[8,128]{1,0:T(8,128)S(1)}) custom-call(f32[256,512]{1,0:T(8,128)S(1)} %copy-done.1, s32[256,1]{1,0:T(8,128)S(1)} %copy.9.owner_ref, s32[1,256]{1,0:T(1,128)S(1)} %bitcast.4, s32[1,256]{1,0:T(1,128)S(1)} %bitcast.5, f32[512,512]{1,0:T(8,128)S(1)} %copy-done, s32[1,512]{1,0:T(1,128)S(1)} %copy-done.2, ...), custom_call_target="tpu_custom_call" | custom-call | tf_op jit(solution)/shard_map/pallas_call | solution.py:383
  74.4 0.5 slice.3
  75.6 0.6 broadcast_divide_fusion
Async XLA Ops:
  0.6 0.7 copy-start.6
  1.3 0.7 copy-start.2
  1.3 0.7 copy-start.3
  1.3 0.7 copy-start.4
  1.3 0.7 copy-start.5
  2.0 1.2 %copy-start = (f32[512,512]{1,0:T(8,128)S(1)}, f32[512,512]{1,0:T(8,128)}, u32[]{:S(2)}) copy-start(f32[512,512]{1,0:T(8,128)} %env_ref.1) | copy-start | bytes 3145732
  3.3 1.0 %copy-start.1 = (f32[256,512]{1,0:T(8,128)S(1)}, f32[256,512]{1,0:T(8,128)}, u32[]{:S(2)}) copy-start(f32[256,512]{1,0:T(8,128)} %rows_ref.1) | copy-start | bytes 1572868

commit v7 on v6

--- a/solution.py
+++ b/solution.py
@@ -377,7 +377,7 @@
     cap = (cap + 15) // 16 * 16
     slots = tiles * cap
     count = 2 * tiles
-    parts = 2 if step % 32 == 0 else 1
+    parts = 4 if step % 64 == 0 else 1
     bits = tiles // 2 * parts
     vmem, dma = pltpu.VMEM, pltpu.SemaphoreType.DMA
     block, square = pl.pallas_call(

time: 77.7 us -> 76.6 us (0.986)
  Pallas kernels: 70.1 us -> 69 us
    pallas_call x1, Pallas kernels: 70.1 us -> 69 us  [body(): pl.pallas_call(functools.partial(kernel, tiles, cap, parts), out_shape=(j...]
where the time goes in v7:
time: 76.6 us; the launch traced here: 76.4 us
  Pallas kernels  69 us (90%)
  local copies, waits for them, and re-layouts  4.16 us (5%)
  between operations  2.53 us (3%)
    pallas_call x1, Pallas kernels, body(): pl.pallas_call(functools.partial(kernel, tiles, cap, parts), out_shape=(j...  69 us
    unnamed x15, local copies, waits for them, and re-layouts  3.65 us

profile of v7, /device:TPU:0, one launch (start us, length us, event | category | flops | bytes accessed | tf_op | source)
XLA Modules:
  0.0 76.4 jit_solution(6562182905841372708)
XLA Ops:
  0.6 0.0 copy-start.6
  0.6 0.7 copy-done.6
  1.3 0.0 copy-start.2
  1.3 0.0 copy-start.3
  1.3 0.0 copy-start.4
  1.3 0.0 copy-start.5
  1.3 0.1 copy.9.owner_ref
  1.5 0.5 copy-done.2
  2.0 0.0 copy-done.3
  2.0 0.0 copy-done.4
  2.0 0.0 copy-done.5
  2.0 0.0 copy-start
  2.0 1.2 %copy-done = f32[512,512]{1,0:T(8,128)S(1)} copy-done((f32[512,512]{1,0:T(8,128)S(1)}, f32[512,512]{1,0:T(8,128)}, u32[]{:S(2)}) %copy-start) | copy-done | bytes 1048600
  3.3 0.0 copy-start.1
  3.3 1.0 %copy-done.1 = f32[256,512]{1,0:T(8,128)S(1)} copy-done((f32[256,512]{1,0:T(8,128)S(1)}, f32[256,512]{1,0:T(8,128)}, u32[]{:S(2)}) %copy-start.1) | copy-done | bytes 524312
  4.3 69.0 %shard_map.86 = (f32[64,256]{1,0:T(8,128)S(1)}, f32[8,128]{1,0:T(8,128)S(1)}) custom-call(f32[256,512]{1,0:T(8,128)S(1)} %copy-done.1, s32[256,1]{1,0:T(8,128)S(1)} %copy.9.owner_ref, s32[1,256]{1,0:T(1,128)S(1)} %bitcast.4, s32[1,256]{1,0:T(1,128)S(1)} %bitcast.5, f32[512,512]{1,0:T(8,128)S(1)} %copy-done, s32[1,512]{1,0:T(1,128)S(1)} %copy-done.2, ...), custom_call_target="tpu_custom_call" | custom-call | tf_op jit(solution)/shard_map/pallas_call | solution.py:383
  73.4 0.5 slice.3
  74.6 0.6 broadcast_divide_fusion
Async XLA Ops:
  0.6 0.7 copy-start.6
  1.3 0.7 copy-start.2
  1.3 0.7 copy-start.3
  1.3 0.7 copy-start.4
  1.3 0.7 copy-start.5
  2.0 1.2 %copy-start = (f32[512,512]{1,0:T(8,128)S(1)}, f32[512,512]{1,0:T(8,128)}, u32[]{:S(2)}) copy-start(f32[512,512]{1,0:T(8,128)} %env_ref.1) | copy-start | bytes 3145732
  3.3 1.0 %copy-start.1 = (f32[256,512]{1,0:T(8,128)S(1)}, f32[256,512]{1,0:T(8,128)}, u32[]{:S(2)}) copy-start(f32[256,512]{1,0:T(8,128)} %rows_ref.1) | copy-start | bytes 1572868

commit v8 on v7

--- a/solution.py
+++ b/solution.py
@@ -135,10 +135,14 @@
                 remote(out_ids.at[both], in_ids.at[:, source], route_send.at[1, pair],
                        route_recv.at[1, source], to, cut))
 
-    @pl.loop(1, pairs)
+    @pl.loop(0, pairs)
     def _(d):
-        for copy in route(lax.rem(pair_me + d, pairs), me):
-            copy.start()
+        pair = lax.rem(pair_me + pairs // 2 + d, pairs)
+
+        @pl.when(pair != pair_me)
+        def _():
+            for copy in route(pair, me):
+                copy.start()
 
     @pl.when(jnp.logical_not(host))
     def _():

time: 76.6 us -> 74.9 us (0.978)
  Pallas kernels: 69 us -> 67.3 us
    pallas_call x1, Pallas kernels: 69 us -> 67.3 us  [body(): pl.pallas_call(functools.partial(kernel, tiles, cap, parts), out_shape=(j...]
where the time goes in v8:
time: 74.9 us; the launch traced here: 74.7 us
  Pallas kernels  67.3 us (90%)
  local copies, waits for them, and re-layouts  4.16 us (6%)
  between operations  2.53 us (3%)
    pallas_call x1, Pallas kernels, body(): pl.pallas_call(functools.partial(kernel, tiles, cap, parts), out_shape=(j...  67.3 us
    unnamed x15, local copies, waits for them, and re-layouts  3.65 us

profile of v8, /device:TPU:0, one launch (start us, length us, event | category | flops | bytes accessed | tf_op | source)
XLA Modules:
  0.0 74.7 jit_solution(16971124616589902408)
XLA Ops:
  0.6 0.0 copy-start.6
  0.6 0.7 copy-done.6
  1.3 0.0 copy-start.2
  1.3 0.0 copy-start.3
  1.3 0.0 copy-start.4
  1.3 0.0 copy-start.5
  1.3 0.1 copy.9.owner_ref
  1.5 0.5 copy-done.2
  2.0 0.0 copy-done.3
  2.0 0.0 copy-done.4
  2.0 0.0 copy-done.5
  2.0 0.0 copy-start
  2.0 1.2 %copy-done = f32[512,512]{1,0:T(8,128)S(1)} copy-done((f32[512,512]{1,0:T(8,128)S(1)}, f32[512,512]{1,0:T(8,128)}, u32[]{:S(2)}) %copy-start) | copy-done | bytes 1048600
  3.3 0.0 copy-start.1
  3.3 1.0 %copy-done.1 = f32[256,512]{1,0:T(8,128)S(1)} copy-done((f32[256,512]{1,0:T(8,128)S(1)}, f32[256,512]{1,0:T(8,128)}, u32[]{:S(2)}) %copy-start.1) | copy-done | bytes 524312
  4.3 67.3 %shard_map.86 = (f32[64,256]{1,0:T(8,128)S(1)}, f32[8,128]{1,0:T(8,128)S(1)}) custom-call(f32[256,512]{1,0:T(8,128)S(1)} %copy-done.1, s32[256,1]{1,0:T(8,128)S(1)} %copy.9.owner_ref, s32[1,256]{1,0:T(1,128)S(1)} %bitcast.4, s32[1,256]{1,0:T(1,128)S(1)} %bitcast.5, f32[512,512]{1,0:T(8,128)S(1)} %copy-done, s32[1,512]{1,0:T(1,128)S(1)} %copy-done.2, ...), custom_call_target="tpu_custom_call" | custom-call | tf_op jit(solution)/shard_map/pallas_call | solution.py:387
  71.6 0.5 slice.3
  72.9 0.6 broadcast_divide_fusion
Async XLA Ops:
  0.6 0.7 copy-start.6
  1.3 0.7 copy-start.2
  1.3 0.7 copy-start.3
  1.3 0.7 copy-start.4
  1.3 0.7 copy-start.5
  2.0 1.2 %copy-start = (f32[512,512]{1,0:T(8,128)S(1)}, f32[512,512]{1,0:T(8,128)}, u32[]{:S(2)}) copy-start(f32[512,512]{1,0:T(8,128)} %env_ref.1) | copy-start | bytes 3145732
  3.3 1.0 %copy-start.1 = (f32[256,512]{1,0:T(8,128)S(1)}, f32[256,512]{1,0:T(8,128)}, u32[]{:S(2)}) copy-start(f32[256,512]{1,0:T(8,128)} %rows_ref.1) | copy-start | bytes 1572868
